TPU v7x, 128 devices: a whole 4x4x4 slice. The times are simulated.
128 devices in a mesh: segment: 8 (over y, core), dp: 16 (over z, x).
Axes of the slice: x: 4, y: 4, z: 4, core: 2. Of those that a mesh axis runs over, the one named last changes fastest.
Arguments:
- tokens: bfloat16 [4096, 1280], P('dp'), may hold values from -6 to 6
- grad_out: bfloat16 [4096, 1280], P('dp'), may hold values from -6 to 6
- first_weight: bfloat16 [8, 1280, 1280], P('segment', 'dp'), may hold values from -0.15625 to 0.15625
- second_weight: bfloat16 [8, 1280, 1280], P('segment', 'dp'), may hold values from -0.15625 to 0.15625
- emb_table: float32 [1000, 1280], replicated, may hold values from -6 to 6
- level_scale: float32 [4, 1280], replicated, may hold values from 0.3 to 3
- timesteps: int32 [32], P('dp'), may hold values from 0 to 999
- levels: int32 [8], P('segment'), may hold values from 0 to 3
Outputs:
- first_grad: float32 [8, 1280, 1280], P('segment', 'dp')
- second_grad: float32 [8, 1280, 1280], P('segment', 'dp')
- input_grads: bfloat16 [8, 4096, 1280], P('segment', 'dp')
All inputs are finite; a program needn't handle non-finite values.
Results may differ from a plain program's by a relative error of at most 0.025.
Values may be sent and summed in bfloat16 or wider, within the bound.
A program may use at most 64 MiB of HBM per device.

v0:
```python
import jax
import jax.numpy as jnp
from jax import lax
from jax.sharding import PartitionSpec as P

epsilon = 1e-06


def shifted(value, axis, steps):
    count = lax.axis_size(axis)
    leading, last = (max(0, -steps), min(count, count - steps))
    return lax.ppermute(value, axis, [(source, source + steps) for source in range(leading, last)])


def partner(block, axis, apart):
    count = lax.axis_size(axis)
    route = []
    for low in range(count):
        high = low | 1 << apart
        if high != low and high < count:
            route += [(low, high), (high, low)]
    return lax.ppermute(block, axis, route)


def normalize(values):
    return values * lax.rsqrt(jnp.mean(values * values, axis=-1, keepdims=True) + epsilon)


def silu_slope(preact):
    sigmoid_value = jax.nn.sigmoid(preact)
    return sigmoid_value * (1.0 + preact * (1.0 - sigmoid_value))


def times_transpose(left, right):
    return lax.dot_general(
        left, right, (((1,), (1,)), ((), ())), preferred_element_type=jnp.float32
    )


def columns_product(left, right):
    return lax.dot_general(
        left, right, (((0,), (0,)), ((), ())), preferred_element_type=jnp.float32
    )


def local(tokens, grad_out, first_weight, second_weight, emb_table, level_scale, timesteps, levels):
    segment_count = lax.axis_size("segment")
    segment_index = lax.axis_index("segment")
    mid_segment = segment_count // 2
    bit_total = segment_count.bit_length() - 1
    row_count, channels = tokens.shape
    gathered_first, gathered_second = (
        lax.all_gather(first_weight, "dp", axis=1, tiled=True),
        lax.all_gather(second_weight, "dp", axis=1, tiled=True),
    )
    first_full = gathered_first[0]
    second_full = gathered_second[0]
    step_picks = (
        timesteps[:, None] == jnp.arange(emb_table.shape[0], dtype=jnp.int32)[None, :]
    ).astype(jnp.float32)
    sample_rows = jnp.dot(step_picks, emb_table, precision=lax.Precision.HIGHEST)
    level_picks = (
        levels[:, None] == jnp.arange(level_scale.shape[0], dtype=jnp.int32)[None, :]
    ).astype(jnp.float32)
    level_row = jnp.dot(level_picks, level_scale, precision=lax.Precision.HIGHEST)
    cond_rows = jnp.repeat(sample_rows * level_row, row_count // timesteps.shape[0], axis=0)
    block_count = 1
    block_rows = row_count // block_count
    last_step = segment_count + block_count - 1
    zeros_bf = jnp.zeros((row_count, channels), jnp.bfloat16)
    zeros_block = jnp.zeros((block_rows, channels), jnp.bfloat16)

    def forward_step(step_number, carry):
        received, skip_in, saved_x, saved_n, saved_z, saved_h, own_out = carry
        micro_block = step_number - segment_index
        active = (micro_block >= 0) & (micro_block < block_count)

        def forward_compute_segment(buffers):
            joined = (received.astype(jnp.float32) + skip_in.astype(jnp.float32)).astype(
                jnp.bfloat16
            )
            segment_input = jnp.where(segment_index == 0, tokens, joined)
            mixed_input = segment_input.astype(jnp.float32) + cond_rows
            normed = normalize(mixed_input).astype(jnp.bfloat16)
            preact = jnp.dot(normed, first_full, preferred_element_type=jnp.float32)
            hidden = jax.nn.silu(preact).astype(jnp.bfloat16)
            result = (
                segment_input.astype(jnp.float32)
                + jnp.dot(hidden, second_full, preferred_element_type=jnp.float32)
            ).astype(jnp.bfloat16)
            return (segment_input, normed, preact, hidden, result, result)

        def forward_unchanged(buffers):
            return buffers + (zeros_block,)

        outcome = lax.cond(
            active,
            forward_compute_segment,
            forward_unchanged,
            (saved_x, saved_n, saved_z, saved_h, own_out),
        )
        received = shifted(outcome[5], "segment", 1)
        return (received, skip_in) + tuple(outcome[:5])

    carry = (
        zeros_block,
        zeros_bf,
        zeros_bf,
        zeros_bf,
        jnp.zeros((row_count, channels), jnp.float32),
        zeros_bf,
        zeros_bf,
    )
    carry = lax.fori_loop(0, mid_segment + 1, forward_step, carry)
    mirrored = carry[6]
    for bit_number in range(bit_total):
        mirrored = partner(mirrored, "segment", bit_number)
    skip_in = jnp.where(segment_index > mid_segment, mirrored, zeros_bf)
    carry = (carry[0], skip_in) + tuple(carry[2:])
    carry = lax.fori_loop(mid_segment + 1, last_step, forward_step, carry)
    saved_x, saved_n, saved_z, saved_h = (carry[2], carry[3], carry[4], carry[5])

    def backward_step(step_number, carry):
        received, skip_grad, saved_gy, saved_dz, saved_dx = carry
        micro_block = step_number - (segment_count - 1 - segment_index)
        active = (micro_block >= 0) & (micro_block < block_count)

        def backward_compute_segment(buffers):
            joined = (received.astype(jnp.float32) + skip_grad.astype(jnp.float32)).astype(
                jnp.bfloat16
            )
            output_grad = jnp.where(segment_index == segment_count - 1, grad_out, joined)
            hidden_grad = times_transpose(output_grad, second_full)
            preact_grad = (hidden_grad * silu_slope(saved_z)).astype(jnp.bfloat16)
            normed_grad = times_transpose(preact_grad, first_full)
            mixed_input = saved_x.astype(jnp.float32) + cond_rows
            pullback = jax.vjp(normalize, mixed_input)[1]
            mixed_grad = pullback(normed_grad)[0]
            input_grad = (output_grad.astype(jnp.float32) + mixed_grad).astype(jnp.bfloat16)
            return (output_grad, preact_grad, input_grad, input_grad)

        def backward_unchanged(buffers):
            return buffers + (zeros_block,)

        outcome = lax.cond(
            active, backward_compute_segment, backward_unchanged, (saved_gy, saved_dz, saved_dx)
        )
        received = shifted(outcome[3], "segment", -1)
        return (received, skip_grad) + tuple(outcome[:3])

    carry = (zeros_block, zeros_bf, zeros_bf, zeros_bf, zeros_bf)
    carry = lax.fori_loop(0, mid_segment + 1, backward_step, carry)
    mirrored_grad = carry[4]
    for bit_number in range(bit_total):
        mirrored_grad = partner(mirrored_grad, "segment", bit_number)
    skip_grad = jnp.where(segment_index < mid_segment - 1, mirrored_grad, zeros_bf)
    carry = (carry[0], skip_grad) + tuple(carry[2:])
    carry = lax.fori_loop(mid_segment + 1, last_step, backward_step, carry)
    saved_gy, saved_dz, saved_dx = (carry[2], carry[3], carry[4])
    first_term = columns_product(saved_n, saved_dz)
    second_term = columns_product(saved_h, saved_gy)
    shares = lax.psum_scatter(
        jnp.concatenate([first_term, second_term], axis=1).astype(jnp.bfloat16),
        "dp",
        scatter_dimension=0,
        tiled=True,
    ).astype(jnp.float32)
    first_grad = shares[:, :channels][None]
    second_grad = shares[:, channels:][None]
    return (first_grad, second_grad, saved_dx[None])


def solution(mesh):
    in_specs = (
        P("dp", None),
        P("dp", None),
        P("segment", "dp", None),
        P("segment", "dp", None),
        P(),
        P(),
        P("dp"),
        P("segment"),
    )
    out_specs = (P("segment", "dp", None), P("segment", "dp", None), P("segment", "dp", None))
    return jax.shard_map(local, mesh=mesh, in_specs=in_specs, out_specs=out_specs, check_vma=False)
```

profile of v0, /device:TPU:0, one launch (start us, length us, event | category | flops | bytes accessed | tf_op | source)
XLA Modules:
  0.0 660.7 jit_solution(4864351868401757183)
XLA Ops:
  9.5 4.2 convolution_multiply_fusion.2
  13.8 47.4 %all-gather.3.cloned.1.call-done = bf16[1,1280,1280]{2,1,0:T(8,128)(2,1)} async-done(((bf16[1,80,1280]{2,1,0:T(8,128)(2,1)}), bf16[1,1280,1280]{2,1,0:T(8,128)(2,1)}) %all-gather.3.cloned.1.call-update) | async-done | bytes 3276816 | tf_op jit(solution)/shard_map/all_gather | solution.py:53
  61.2 49.4 %all-gather.5.cloned.1.call-done = bf16[1,1280,1280]{2,1,0:T(8,128)(2,1)} async-done(((bf16[1,80,1280]{2,1,0:T(8,128)(2,1)}), bf16[1,1280,1280]{2,1,0:T(8,128)(2,1)}) %all-gather.5.cloned.1.call-update) | async-done | bytes 3276816 | tf_op jit(solution)/shard_map/all_gather | solution.py:54
  110.5 1.2 broadcast_in_dim.20
  116.2 90.0 %while.88 = (s32[]{:T(128)}, bf16[256,1280]{1,0:T(8,128)(2,1)}, bf16[256,1280]{1,0:T(8,128)(2,1)}, bf16[256,1280]{1,0:T(8,128)(2,1)}, f32[256,1280]{1,0:T(8,128)...) while((s32[]{:T(128)}, bf16[256,1280]{1,0:T(8,128)(2,1)}, ...), condition=%wide.region_4.5_spmd.clone, body=%wide.region_0.4_spmd.clone.sunk | while | flops 1683292416 | bytes 40647064 | solution.py:114
  117.4 13.5 %conditional.12 = (bf16[256,1280]{1,0:T(8,128)(2,1)}, bf16[256,1280]{1,0:T(8,128)(2,1)}, f32[256,1280]{1,0:T(8,128)}, bf16[256,1280]{1,0:T(8,128)(2,1)}, bf16[25...) conditional(s32[]{:T(128)} %convert_element_type.180, (bf16[256,1280]{1,0:T(8,128)(2,1)}, ...), branch_computations={%region_1.0_spmd, %region_2.3_spmd} | conditional | flops 1683292416 | bytes 36704368 | solution.py:96
  117.4 2.7 multiply_reduce_fusion
  120.1 2.1 multiply_convert_fusion.1
  122.2 3.5 multiply_convert_fusion
  125.8 3.1 fusion.8
  128.9 2.0 copy.28
  130.9 2.2 collective-permute-start
  136.3 15.8 %collective-permute-start = (bf16[256,1280]{1,0:T(8,128)(2,1)}, bf16[256,1280]{1,0:T(8,128)(2,1)}, u32[]{:S(2)}, u32[]{:S(2)}) collective-permute-start(bf16[256,1280]{1,0:T(8,128)(2,1)} %get-tuple-element.1695), channel_id=1, source_target_pairs={{0,16},{16,32},{32,48},{48,64},{64,80},{80,96},{96,112},{1,17},{17... | collective-permute-start | bytes 1966088 | tf_op jit(solution)/shard_map/while/body/eval_jaxpr/ppermute | solution.py:12
  152.1 1.2 collective-permute-done
  155.3 8.6 %collective-permute-start = (bf16[256,1280]{1,0:T(8,128)(2,1)}, bf16[256,1280]{1,0:T(8,128)(2,1)}, u32[]{:S(2)}, u32[]{:S(2)}) collective-permute-start(bf16[256,1280]{1,0:T(8,128)(2,1)} %get-tuple-element.1695), channel_id=1, source_target_pairs={{0,16},{16,32},{32,48},{48,64},{64,80},{80,96},{96,112},{1,17},{17... | collective-permute-start | bytes 1966088 | tf_op jit(solution)/shard_map/while/body/eval_jaxpr/ppermute | solution.py:12
  167.1 23.7 %collective-permute-start = (bf16[256,1280]{1,0:T(8,128)(2,1)}, bf16[256,1280]{1,0:T(8,128)(2,1)}, u32[]{:S(2)}, u32[]{:S(2)}) collective-permute-start(bf16[256,1280]{1,0:T(8,128)(2,1)} %get-tuple-element.1695), channel_id=1, source_target_pairs={{0,16},{16,32},{32,48},{48,64},{64,80},{80,96},{96,112},{1,17},{17... | collective-permute-start | bytes 1966088 | tf_op jit(solution)/shard_map/while/body/eval_jaxpr/ppermute | solution.py:12
  194.0 11.1 %collective-permute-start = (bf16[256,1280]{1,0:T(8,128)(2,1)}, bf16[256,1280]{1,0:T(8,128)(2,1)}, u32[]{:S(2)}, u32[]{:S(2)}) collective-permute-start(bf16[256,1280]{1,0:T(8,128)(2,1)} %get-tuple-element.1695), channel_id=1, source_target_pairs={{0,16},{16,32},{32,48},{48,64},{64,80},{80,96},{96,112},{1,17},{17... | collective-permute-start | bytes 1966088 | tf_op jit(solution)/shard_map/while/body/eval_jaxpr/ppermute | solution.py:12
  206.2 8.3 %collective-permute-start.4 = (bf16[256,1280]{1,0:T(8,128)(2,1)}, bf16[256,1280]{1,0:T(8,128)(2,1)S(1)}, u32[]{:S(2)}, u32[]{:S(2)}) collective-permute-start(bf16[256,1280]{1,0:T(8,128)(2,1)} %get-tuple-element.1132), channel_id=1, source_target_pairs={{0,16},{16,0},{32,48},{48,32},{64,80},{80,64},{96,112},{112,96},{1... | collective-permute-start | bytes 1966088 | tf_op jit(solution)/shard_map/ppermute | solution.py:22
  214.5 1.9 collective-permute-done.4
  216.4 17.3 %collective-permute-start.5 = (bf16[256,1280]{1,0:T(8,128)(2,1)S(1)}, bf16[256,1280]{1,0:T(8,128)(2,1)}, u32[]{:S(2)}, u32[]{:S(2)}) collective-permute-start(bf16[256,1280]{1,0:T(8,128)(2,1)S(1)} %collective-permute-done.4), channel_id=1, source_target_pairs={{0,32},{32,0},{16,48},{48,16},{64,96},{96,64},{80,112},{112,80},{1... | collective-permute-start | bytes 1966088 | tf_op jit(solution)/shard_map/ppermute | solution.py:22
  233.7 15.4 %collective-permute-done.5 = bf16[256,1280]{1,0:T(8,128)(2,1)} collective-permute-done((bf16[256,1280]{1,0:T(8,128)(2,1)S(1)}, bf16[256,1280]{1,0:T(8,128)(2,1)}, u32[]{:S(2)}, u32[]{:S(2)}) %collective-permute-start.5) | collective-permute-done | bytes 655392 | tf_op jit(solution)/shard_map/ppermute | solution.py:22
  249.1 4.3 collective-permute-start.6
  253.4 14.5 %collective-permute-done.6 = bf16[256,1280]{1,0:T(8,128)(2,1)} collective-permute-done((bf16[256,1280]{1,0:T(8,128)(2,1)}, bf16[256,1280]{1,0:T(8,128)(2,1)}, u32[]{:S(2)}, u32[]{:S(2)}) %collective-permute-start.6) | collective-permute-done | bytes 655392 | tf_op jit(solution)/shard_map/ppermute | solution.py:22
  268.8 33.1 %while.89 = (s32[]{:T(128)}, bf16[256,1280]{1,0:T(8,128)(2,1)}, bf16[256,1280]{1,0:T(8,128)(2,1)}, bf16[256,1280]{1,0:T(8,128)(2,1)}, f32[256,1280]{1,0:T(8,128)...) while((s32[]{:T(128)}, bf16[256,1280]{1,0:T(8,128)(2,1)}, ...), condition=%wide.region_9.10_spmd.clone, body=%wide.region_5.9_spmd.clone.sunk | while | flops 1684603136 | bytes 39991720 | solution.py:120
  270.8 2.2 collective-permute-start.1
  276.2 10.3 %collective-permute-start.1 = (bf16[256,1280]{1,0:T(8,128)(2,1)}, bf16[256,1280]{1,0:T(8,128)(2,1)}, u32[]{:S(2)}, u32[]{:S(2)}) collective-permute-start(bf16[256,1280]{1,0:T(8,128)(2,1)} %get-tuple-element.1713), channel_id=1, source_target_pairs={{0,16},{16,32},{32,48},{48,64},{64,80},{80,96},{96,112},{1,17},{17... | collective-permute-start | bytes 1966088 | tf_op jit(solution)/shard_map/while/body/eval_jaxpr/ppermute | solution.py:12
  289.6 11.1 %collective-permute-start.1 = (bf16[256,1280]{1,0:T(8,128)(2,1)}, bf16[256,1280]{1,0:T(8,128)(2,1)}, u32[]{:S(2)}, u32[]{:S(2)}) collective-permute-start(bf16[256,1280]{1,0:T(8,128)(2,1)} %get-tuple-element.1713), channel_id=1, source_target_pairs={{0,16},{16,32},{32,48},{48,64},{64,80},{80,96},{96,112},{1,17},{17... | collective-permute-start | bytes 1966088 | tf_op jit(solution)/shard_map/while/body/eval_jaxpr/ppermute | solution.py:12
  305.5 74.9 %while.90 = (s32[]{:T(128)}, bf16[256,1280]{1,0:T(8,128)(2,1)}, bf16[256,1280]{1,0:T(8,128)(2,1)}, bf16[256,1280]{1,0:T(8,128)(2,1)}, bf16[256,1280]{1,0:T(8,128...) while((s32[]{:T(128)}, bf16[256,1280]{1,0:T(8,128)(2,1)}, ...), condition=%wide.region_15.0_spmd.clone, body=%wide.region_10.15_spmd.clone.sunk | while | flops 1685914624 | bytes 30165368 | solution.py:152
  307.5 1.3 collective-permute-start.2
  308.8 10.8 %collective-permute-done.2 = bf16[256,1280]{1,0:T(8,128)(2,1)} collective-permute-done((bf16[256,1280]{1,0:T(8,128)(2,1)}, bf16[256,1280]{1,0:T(8,128)(2,1)}, u32[]{:S(2)}, u32[]{:S(2)}) %collective-permute-start.2) | collective-permute-done | bytes 655392 | tf_op jit(solution)/shard_map/while/body/eval_jaxpr/ppermute | solution.py:12
  321.6 1.3 collective-permute-start.2
  322.9 11.7 %collective-permute-done.2 = bf16[256,1280]{1,0:T(8,128)(2,1)} collective-permute-done((bf16[256,1280]{1,0:T(8,128)(2,1)}, bf16[256,1280]{1,0:T(8,128)(2,1)}, u32[]{:S(2)}, u32[]{:S(2)}) %collective-permute-start.2) | collective-permute-done | bytes 655392 | tf_op jit(solution)/shard_map/while/body/eval_jaxpr/ppermute | solution.py:12
  336.6 1.3 collective-permute-start.2
  337.9 10.9 %collective-permute-done.2 = bf16[256,1280]{1,0:T(8,128)(2,1)} collective-permute-done((bf16[256,1280]{1,0:T(8,128)(2,1)}, bf16[256,1280]{1,0:T(8,128)(2,1)}, u32[]{:S(2)}, u32[]{:S(2)}) %collective-permute-start.2) | collective-permute-done | bytes 655392 | tf_op jit(solution)/shard_map/while/body/eval_jaxpr/ppermute | solution.py:12
  350.9 1.3 collective-permute-start.2
  352.2 13.9 %collective-permute-done.2 = bf16[256,1280]{1,0:T(8,128)(2,1)} collective-permute-done((bf16[256,1280]{1,0:T(8,128)(2,1)}, bf16[256,1280]{1,0:T(8,128)(2,1)}, u32[]{:S(2)}, u32[]{:S(2)}) %collective-permute-start.2) | collective-permute-done | bytes 655392 | tf_op jit(solution)/shard_map/while/body/eval_jaxpr/ppermute | solution.py:12
  368.1 1.3 collective-permute-start.2
  369.4 10.9 %collective-permute-done.2 = bf16[256,1280]{1,0:T(8,128)(2,1)} collective-permute-done((bf16[256,1280]{1,0:T(8,128)(2,1)}, bf16[256,1280]{1,0:T(8,128)(2,1)}, u32[]{:S(2)}, u32[]{:S(2)}) %collective-permute-start.2) | collective-permute-done | bytes 655392 | tf_op jit(solution)/shard_map/while/body/eval_jaxpr/ppermute | solution.py:12
  380.3 9.0 %collective-permute-start.7 = (bf16[256,1280]{1,0:T(8,128)(2,1)}, bf16[256,1280]{1,0:T(8,128)(2,1)S(1)}, u32[]{:S(2)}, u32[]{:S(2)}) collective-permute-start(bf16[256,1280]{1,0:T(8,128)(2,1)} %get-tuple-element.1927), channel_id=1, source_target_pairs={{0,16},{16,0},{32,48},{48,32},{64,80},{80,64},{96,112},{112,96},{1... | collective-permute-start | bytes 1966088 | tf_op jit(solution)/shard_map/ppermute | solution.py:22
  389.3 1.9 collective-permute-done.7
  391.3 59.7 %collective-permute-start.8 = (bf16[256,1280]{1,0:T(8,128)(2,1)S(1)}, bf16[256,1280]{1,0:T(8,128)(2,1)}, u32[]{:S(2)}, u32[]{:S(2)}) collective-permute-start(bf16[256,1280]{1,0:T(8,128)(2,1)S(1)} %collective-permute-done.7), channel_id=1, source_target_pairs={{0,32},{32,0},{16,48},{48,16},{64,96},{96,64},{80,112},{112,80},{1... | collective-permute-start | bytes 1966088 | tf_op jit(solution)/shard_map/ppermute | solution.py:22
  451.0 15.4 %collective-permute-done.8 = bf16[256,1280]{1,0:T(8,128)(2,1)} collective-permute-done((bf16[256,1280]{1,0:T(8,128)(2,1)S(1)}, bf16[256,1280]{1,0:T(8,128)(2,1)}, u32[]{:S(2)}, u32[]{:S(2)}) %collective-permute-start.8) | collective-permute-done | bytes 655392 | tf_op jit(solution)/shard_map/ppermute | solution.py:22
  466.4 1.6 collective-permute-start.9
  468.0 16.6 %collective-permute-done.9 = bf16[256,1280]{1,0:T(8,128)(2,1)} collective-permute-done((bf16[256,1280]{1,0:T(8,128)(2,1)}, bf16[256,1280]{1,0:T(8,128)(2,1)}, u32[]{:S(2)}, u32[]{:S(2)}) %collective-permute-start.9) | collective-permute-done | bytes 655392 | tf_op jit(solution)/shard_map/ppermute | solution.py:22
  484.6 2.0 broadcast_select_fusion.2
  486.6 65.5 %while.91 = (s32[]{:T(128)}, bf16[256,1280]{1,0:T(8,128)(2,1)}, bf16[256,1280]{1,0:T(8,128)(2,1)}, bf16[256,1280]{1,0:T(8,128)(2,1)}, bf16[256,1280]{1,0:T(8,128...) while((s32[]{:T(128)}, bf16[256,1280]{1,0:T(8,128)(2,1)}, ...), condition=%wide.region_21.0_spmd.clone, body=%wide.region_16.21_spmd.clone.sunk | while | flops 1687225344 | bytes 30820764 | solution.py:158
  488.6 1.3 collective-permute-start.3
  489.9 3.0 collective-permute-done.3
  495.0 1.3 collective-permute-start.3
  496.3 36.4 %collective-permute-done.3 = bf16[256,1280]{1,0:T(8,128)(2,1)} collective-permute-done((bf16[256,1280]{1,0:T(8,128)(2,1)}, bf16[256,1280]{1,0:T(8,128)(2,1)}, u32[]{:S(2)}, u32[]{:S(2)}) %collective-permute-start.3) | collective-permute-done | bytes 655392 | tf_op jit(solution)/shard_map/while/body/eval_jaxpr/ppermute | solution.py:12
  533.9 14.0 %conditional.15 = (bf16[256,1280]{1,0:T(8,128)(2,1)}, bf16[256,1280]{1,0:T(8,128)(2,1)}, bf16[256,1280]{1,0:T(8,128)(2,1)}, bf16[256,1280]{1,0:T(8,128)(2,1)}) conditional(s32[]{:T(128)} %convert_element_type.183, (bf16[256,1280]{1,0:T(8,128)(2,1)}, bf16[256,1280]{1,0:T(8,128)(2,1)}, bf16[256,1280]{1,0:T(8,128)(2,1)}) %tuple.188, (s32[]{:T(128)}, ...), branch_computations={%region_17.17_spmd, %region_18.0_spmd} | conditional | flops 1687225344 | bytes 26878022 | solution.py:145
  533.9 2.4 fusion.18
  536.2 4.5 fusion.15
  540.7 2.5 multiply_reduce_fusion.5
  543.3 2.6 fusion.17
  545.8 2.0 copy.54
  547.8 1.3 collective-permute-start.3
  549.1 3.0 collective-permute-done.3
  552.1 2.3 convolution_convert_fusion.1
  554.5 2.4 convolution_convert_fusion
  556.8 3.2 pad_maximum_fusion
  560.0 9.5 %copy.15 = bf16[1280,2560]{1,0:T(8,128)(2,1)} copy(bf16[1280,2560]{0,1:T(8,128)(2,1)} %pad_maximum_fusion) | data formatting | bytes 13107200
  569.6 81.2 %reduce-scatter.4.cloned.1.call-done = bf16[80,2560]{1,0:T(8,128)(2,1)} async-done(((bf16[1280,2560]{1,0:T(8,128)(2,1)}), bf16[80,2560]{1,0:T(8,128)(2,1)}) %reduce-scatter.4.cloned.1.call-update) | async-done | bytes 409616
  650.7 1.3 copy.16
  (84 shorter events, 64.3 us)
Async XLA Ops:
  7.2 2.2 copy-start
  7.2 54.0 %all-gather.3.cloned.1.call-start = ((), (), s32[]{:S(2)}) async-start(), calls=%async_computation.1 | async-start | bytes 3481600 | tf_op jit(solution)/shard_map/all_gather | solution.py:53
  7.9 102.6 %all-gather.5.cloned.1.call-start = ((), (), s32[]{:S(2)}) async-start(), calls=%async_computation.2 | async-start | bytes 3481600 | tf_op jit(solution)/shard_map/all_gather | solution.py:54
  8.7 642.1 %reduce-scatter.4.cloned.1.call-start = ((), (), s32[]{:S(2)}) async-start(), calls=%async_computation.3 | async-start | bytes 6963200
  111.7 4.5 copy-start.1
  117.4 2.8 copy-start.2
  122.2 3.5 copy-start.6
  130.9 3.3 collective-permute-start
  136.3 17.0 %collective-permute-start = (bf16[256,1280]{1,0:T(8,128)(2,1)}, bf16[256,1280]{1,0:T(8,128)(2,1)}, u32[]{:S(2)}, u32[]{:S(2)}) collective-permute-start(bf16[256,1280]{1,0:T(8,128)(2,1)} %get-tuple-element.1695), channel_id=1, source_target_pairs={{0,16},{16,32},{32,48},{48,64},{64,80},{80,96},{96,112},{1,17},{17... | collective-permute-start | bytes 1966088 | tf_op jit(solution)/shard_map/while/body/eval_jaxpr/ppermute | solution.py:12
  155.3 9.7 %collective-permute-start = (bf16[256,1280]{1,0:T(8,128)(2,1)}, bf16[256,1280]{1,0:T(8,128)(2,1)}, u32[]{:S(2)}, u32[]{:S(2)}) collective-permute-start(bf16[256,1280]{1,0:T(8,128)(2,1)} %get-tuple-element.1695), channel_id=1, source_target_pairs={{0,16},{16,32},{32,48},{48,64},{64,80},{80,96},{96,112},{1,17},{17... | collective-permute-start | bytes 1966088 | tf_op jit(solution)/shard_map/while/body/eval_jaxpr/ppermute | solution.py:12
  167.1 24.9 %collective-permute-start = (bf16[256,1280]{1,0:T(8,128)(2,1)}, bf16[256,1280]{1,0:T(8,128)(2,1)}, u32[]{:S(2)}, u32[]{:S(2)}) collective-permute-start(bf16[256,1280]{1,0:T(8,128)(2,1)} %get-tuple-element.1695), channel_id=1, source_target_pairs={{0,16},{16,32},{32,48},{48,64},{64,80},{80,96},{96,112},{1,17},{17... | collective-permute-start | bytes 1966088 | tf_op jit(solution)/shard_map/while/body/eval_jaxpr/ppermute | solution.py:12
  194.0 12.2 %collective-permute-start = (bf16[256,1280]{1,0:T(8,128)(2,1)}, bf16[256,1280]{1,0:T(8,128)(2,1)}, u32[]{:S(2)}, u32[]{:S(2)}) collective-permute-start(bf16[256,1280]{1,0:T(8,128)(2,1)} %get-tuple-element.1695), channel_id=1, source_target_pairs={{0,16},{16,32},{32,48},{48,64},{64,80},{80,96},{96,112},{1,17},{17... | collective-permute-start | bytes 1966088 | tf_op jit(solution)/shard_map/while/body/eval_jaxpr/ppermute | solution.py:12
  206.2 10.2 %collective-permute-start.4 = (bf16[256,1280]{1,0:T(8,128)(2,1)}, bf16[256,1280]{1,0:T(8,128)(2,1)S(1)}, u32[]{:S(2)}, u32[]{:S(2)}) collective-permute-start(bf16[256,1280]{1,0:T(8,128)(2,1)} %get-tuple-element.1132), channel_id=1, source_target_pairs={{0,16},{16,0},{32,48},{48,32},{64,80},{80,64},{96,112},{112,96},{1... | collective-permute-start | bytes 1966088 | tf_op jit(solution)/shard_map/ppermute | solution.py:22
  216.4 32.7 %collective-permute-start.5 = (bf16[256,1280]{1,0:T(8,128)(2,1)S(1)}, bf16[256,1280]{1,0:T(8,128)(2,1)}, u32[]{:S(2)}, u32[]{:S(2)}) collective-permute-start(bf16[256,1280]{1,0:T(8,128)(2,1)S(1)} %collective-permute-done.4), channel_id=1, source_target_pairs={{0,32},{32,0},{16,48},{48,16},{64,96},{96,64},{80,112},{112,80},{1... | collective-permute-start | bytes 1966088 | tf_op jit(solution)/shard_map/ppermute | solution.py:22
  249.1 18.8 %collective-permute-start.6 = (bf16[256,1280]{1,0:T(8,128)(2,1)}, bf16[256,1280]{1,0:T(8,128)(2,1)}, u32[]{:S(2)}, u32[]{:S(2)}) collective-permute-start(bf16[256,1280]{1,0:T(8,128)(2,1)} %collective-permute-done.5), channel_id=1, source_target_pairs={{0,64},{64,0},{16,80},{80,16},{32,96},{96,32},{48,112},{112,48},{1... | collective-permute-start | bytes 1966088 | tf_op jit(solution)/shard_map/ppermute | solution.py:22
  270.8 3.3 collective-permute-start.1
  276.2 11.4 %collective-permute-start.1 = (bf16[256,1280]{1,0:T(8,128)(2,1)}, bf16[256,1280]{1,0:T(8,128)(2,1)}, u32[]{:S(2)}, u32[]{:S(2)}) collective-permute-start(bf16[256,1280]{1,0:T(8,128)(2,1)} %get-tuple-element.1713), channel_id=1, source_target_pairs={{0,16},{16,32},{32,48},{48,64},{64,80},{80,96},{96,112},{1,17},{17... | collective-permute-start | bytes 1966088 | tf_op jit(solution)/shard_map/while/body/eval_jaxpr/ppermute | solution.py:12
  289.6 12.2 %collective-permute-start.1 = (bf16[256,1280]{1,0:T(8,128)(2,1)}, bf16[256,1280]{1,0:T(8,128)(2,1)}, u32[]{:S(2)}, u32[]{:S(2)}) collective-permute-start(bf16[256,1280]{1,0:T(8,128)(2,1)} %get-tuple-element.1713), channel_id=1, source_target_pairs={{0,16},{16,32},{32,48},{48,64},{64,80},{80,96},{96,112},{1,17},{17... | collective-permute-start | bytes 1966088 | tf_op jit(solution)/shard_map/while/body/eval_jaxpr/ppermute | solution.py:12
  307.5 12.1 %collective-permute-start.2 = (bf16[256,1280]{1,0:T(8,128)(2,1)}, bf16[256,1280]{1,0:T(8,128)(2,1)}, u32[]{:S(2)}, u32[]{:S(2)}) collective-permute-start(bf16[256,1280]{1,0:T(8,128)(2,1)} %get-tuple-element.1731), channel_id=1, source_target_pairs={{16,0},{32,16},{48,32},{64,48},{80,64},{96,80},{112,96},{17,1},{33... | collective-permute-start | bytes 1966088 | tf_op jit(solution)/shard_map/while/body/eval_jaxpr/ppermute | solution.py:12
  321.6 13.0 %collective-permute-start.2 = (bf16[256,1280]{1,0:T(8,128)(2,1)}, bf16[256,1280]{1,0:T(8,128)(2,1)}, u32[]{:S(2)}, u32[]{:S(2)}) collective-permute-start(bf16[256,1280]{1,0:T(8,128)(2,1)} %get-tuple-element.1731), channel_id=1, source_target_pairs={{16,0},{32,16},{48,32},{64,48},{80,64},{96,80},{112,96},{17,1},{33... | collective-permute-start | bytes 1966088 | tf_op jit(solution)/shard_map/while/body/eval_jaxpr/ppermute | solution.py:12
  336.6 12.2 %collective-permute-start.2 = (bf16[256,1280]{1,0:T(8,128)(2,1)}, bf16[256,1280]{1,0:T(8,128)(2,1)}, u32[]{:S(2)}, u32[]{:S(2)}) collective-permute-start(bf16[256,1280]{1,0:T(8,128)(2,1)} %get-tuple-element.1731), channel_id=1, source_target_pairs={{16,0},{32,16},{48,32},{64,48},{80,64},{96,80},{112,96},{17,1},{33... | collective-permute-start | bytes 1966088 | tf_op jit(solution)/shard_map/while/body/eval_jaxpr/ppermute | solution.py:12
  350.9 15.2 %collective-permute-start.2 = (bf16[256,1280]{1,0:T(8,128)(2,1)}, bf16[256,1280]{1,0:T(8,128)(2,1)}, u32[]{:S(2)}, u32[]{:S(2)}) collective-permute-start(bf16[256,1280]{1,0:T(8,128)(2,1)} %get-tuple-element.1731), channel_id=1, source_target_pairs={{16,0},{32,16},{48,32},{64,48},{80,64},{96,80},{112,96},{17,1},{33... | collective-permute-start | bytes 1966088 | tf_op jit(solution)/shard_map/while/body/eval_jaxpr/ppermute | solution.py:12
  368.1 12.2 %collective-permute-start.2 = (bf16[256,1280]{1,0:T(8,128)(2,1)}, bf16[256,1280]{1,0:T(8,128)(2,1)}, u32[]{:S(2)}, u32[]{:S(2)}) collective-permute-start(bf16[256,1280]{1,0:T(8,128)(2,1)} %get-tuple-element.1731), channel_id=1, source_target_pairs={{16,0},{32,16},{48,32},{64,48},{80,64},{96,80},{112,96},{17,1},{33... | collective-permute-start | bytes 1966088 | tf_op jit(solution)/shard_map/while/body/eval_jaxpr/ppermute | solution.py:12
  380.3 10.9 %collective-permute-start.7 = (bf16[256,1280]{1,0:T(8,128)(2,1)}, bf16[256,1280]{1,0:T(8,128)(2,1)S(1)}, u32[]{:S(2)}, u32[]{:S(2)}) collective-permute-start(bf16[256,1280]{1,0:T(8,128)(2,1)} %get-tuple-element.1927), channel_id=1, source_target_pairs={{0,16},{16,0},{32,48},{48,32},{64,80},{80,64},{96,112},{112,96},{1... | collective-permute-start | bytes 1966088 | tf_op jit(solution)/shard_map/ppermute | solution.py:22
  391.3 75.1 %collective-permute-start.8 = (bf16[256,1280]{1,0:T(8,128)(2,1)S(1)}, bf16[256,1280]{1,0:T(8,128)(2,1)}, u32[]{:S(2)}, u32[]{:S(2)}) collective-permute-start(bf16[256,1280]{1,0:T(8,128)(2,1)S(1)} %collective-permute-done.7), channel_id=1, source_target_pairs={{0,32},{32,0},{16,48},{48,16},{64,96},{96,64},{80,112},{112,80},{1... | collective-permute-start | bytes 1966088 | tf_op jit(solution)/shard_map/ppermute | solution.py:22
  466.4 18.3 %collective-permute-start.9 = (bf16[256,1280]{1,0:T(8,128)(2,1)}, bf16[256,1280]{1,0:T(8,128)(2,1)}, u32[]{:S(2)}, u32[]{:S(2)}) collective-permute-start(bf16[256,1280]{1,0:T(8,128)(2,1)} %collective-permute-done.8), channel_id=1, source_target_pairs={{0,64},{64,0},{16,80},{80,16},{32,96},{96,32},{48,112},{112,48},{1... | collective-permute-start | bytes 1966088 | tf_op jit(solution)/shard_map/ppermute | solution.py:22
  488.6 4.3 collective-permute-start.3
  495.0 37.7 %collective-permute-start.3 = (bf16[256,1280]{1,0:T(8,128)(2,1)}, bf16[256,1280]{1,0:T(8,128)(2,1)}, u32[]{:S(2)}, u32[]{:S(2)}) collective-permute-start(bf16[256,1280]{1,0:T(8,128)(2,1)} %get-tuple-element.1749), channel_id=1, source_target_pairs={{16,0},{32,16},{48,32},{64,48},{80,64},{96,80},{112,96},{17,1},{33... | collective-permute-start | bytes 1966088 | tf_op jit(solution)/shard_map/while/body/eval_jaxpr/ppermute | solution.py:12
  536.2 4.5 copy-start.5
  547.8 4.3 collective-permute-start.3
Sparse Core Ops, SparseCore 0:
  10.2 50.9 all-gather.2
  63.3 47.1 all-gather.4
  569.7 81.0 reduce-scatter.3
where the time goes:
time: 662 us; the launch traced here: 661 us
  waiting for transfers between devices  355 us (54%)
  starting transfers between devices  195 us (29%)
  local copies, waits for them, and re-layouts  57 us (9%)
  matrix products  22.8 us (3%)
  other arithmetic  16 us (2%)
  between operations  14.5 us (2%)
    ppermute x16, waiting for transfers between devices, shifted(): lax.ppermute(value, axis, [(source, source + steps) for source in range(l...  110 us
    ppermute x6, starting transfers between devices, partner(): return lax.ppermute(block, axis, route)  100 us
    ppermute x16, starting transfers between devices, shifted(): lax.ppermute(value, axis, [(source, source + steps) for source in range(l...  95.1 us
    unnamed x4, waiting for transfers between devices  82.6 us
    ppermute x6, waiting for transfers between devices, partner(): return lax.ppermute(block, axis, route)  65.7 us
    all_gather x1, waiting for transfers between devices, local(): lax.all_gather(second_weight, 'dp', axis=1, tiled=True)  49.4 us
    all_gather x1, waiting for transfers between devices, local(): lax.all_gather(first_weight, 'dp', axis=1, tiled=True)  47.4 us
    another operation x23, local copies, waits for them, and re-layouts  20.7 us
  transfers between devices with their start and end apart: 25, of which 25 were waited for; matrix products, arithmetic and copies ran while one was open for 1% of the time, Pallas kernels for 0%

commit v1 on v0

v1 whole, which is shorter than its diff:
```python
import functools

import jax
import jax.numpy as jnp
from jax import lax
from jax.experimental import pallas as pl
from jax.experimental.pallas import tpu as pltpu
from jax.sharding import PartitionSpec as P

EPS = 1e-06
SECTIONS = 8
RING = 4
BLOCKS = 4
HALVES = ((0, 640), (640, 640))
F32 = jnp.float32
BF = jnp.bfloat16


def dot(a, b, contract):
    return lax.dot_general(a, b, (contract, ((), ())), preferred_element_type=F32)


def kernel(
    tok, go, w1, w2, emb, lvl, ts, lv,
    fg, sg, dxo,
    W1, W2, G1, G2, nT, hT,
    xr, sk, yb, nb, hb, un, sl, gr, gk, dz, dn, dx, rr, cond,
    embv, lvlv, acc1, acc2, r1, r2, r4, r5,
    gsend, grecv, ssend, srecv, psend, precv, lsem,
):
    seg = lax.axis_index("segment")
    dp = lax.axis_index("dp")
    z, x = dp // RING, dp % RING
    rows, chan = xr.shape
    step = rows // BLOCKS
    samples = ts.shape[0]

    def at_z(i):
        return lax.rem(z + i + RING, RING)

    def at_x(i):
        return lax.rem(x + i + RING, RING)

    def dev(axis, i):
        return {"dp": at_z(i) * RING + x} if axis == "z" else {"dp": z * RING + at_x(i)}

    own1 = pltpu.make_async_copy(w1.at[0], W1.at[z, x], lsem.at[0])
    own2 = pltpu.make_async_copy(w2.at[0], W2.at[z, x], lsem.at[1])
    table = pltpu.make_async_copy(emb, embv, lsem.at[2])
    scales = pltpu.make_async_copy(lvl, lvlv, lsem.at[3])
    own1.start()
    own2.start()
    table.start()
    scales.start()
    tok_in = pltpu.make_async_copy(tok, xr, lsem.at[4])
    go_in = pltpu.make_async_copy(go, gr, lsem.at[5])

    @pl.when(seg == 0)
    def _():
        tok_in.start()

    @pl.when(seg == SECTIONS - 1)
    def _():
        go_in.start()

    barrier = pltpu.get_barrier_semaphore()
    for axis in ("z", "x"):
        for way in (1, -1):
            pl.semaphore_signal(barrier, inc=1, device_id=dev(axis, way))

    @pl.when(seg > 0)
    def _():
        pl.semaphore_signal(barrier, inc=1, device_id={"segment": seg - 1})

    @pl.when(seg < SECTIONS - 1)
    def _():
        pl.semaphore_signal(barrier, inc=1, device_id={"segment": seg + 1})

    far = jnp.logical_or(seg < 3, seg > 4)

    @pl.when(far)
    def _():
        pl.semaphore_signal(barrier, inc=1, device_id={"segment": SECTIONS - 1 - seg})

    pl.semaphore_wait(
        barrier,
        4
        + (seg > 0).astype(jnp.int32)
        + (seg < SECTIONS - 1).astype(jnp.int32)
        + far.astype(jnp.int32),
    )
    own1.wait()
    own2.wait()

    units = [(w, h) for w in range(2) for h in range(2)]
    axes = (("x", "z"), ("z", "x"))
    offs = {"x": at_x, "z": at_z}

    def one(ref, h, first, second, part):
        i = (second, first) if h == 0 else (first, second)
        return ref.at[i[0], i[1], part, pl.ds(*HALVES[h])]

    def many(ref, h, second, part):
        if h == 0:
            return ref.at[second, part, :, pl.ds(*HALVES[h])]
        return ref.at[part, second, :, pl.ds(*HALVES[h])]

    ALL, TOP, LOW = pl.ds(0, 80), pl.ds(0, 48), pl.ds(48, 32)
    SUB, SUB0, SUB1 = pl.ds(0, 4), pl.ds(0, 2), pl.ds(2, 2)

    def gcopy(u, kind, ref, axis, way):
        k = u * 8 + kind
        return pltpu.make_async_remote_copy(
            src_ref=ref, dst_ref=ref, send_sem=gsend.at[k], recv_sem=grecv.at[k],
            device_id=dev(axis, way),
        )

    def gather_copy(u, kind):
        w, h = units[u]
        ref = (W1, W2)[w]
        a, b = axes[h]
        pa, pb = offs[a], offs[b]
        return (
            lambda: gcopy(u, 0, one(ref, h, pa(0), pb(0), ALL), a, 1),
            lambda: gcopy(u, 1, one(ref, h, pa(0), pb(0), ALL), a, -1),
            lambda: gcopy(u, 2, one(ref, h, pa(-1), pb(0), TOP), a, 1),
            lambda: gcopy(u, 3, one(ref, h, pa(1), pb(0), LOW), a, -1),
            lambda: gcopy(u, 4, many(ref, h, pb(0), SUB), b, 1),
            lambda: gcopy(u, 5, many(ref, h, pb(0), SUB), b, -1),
            lambda: gcopy(u, 6, many(ref, h, pb(-1), SUB0), b, 1),
            lambda: gcopy(u, 7, many(ref, h, pb(1), SUB1), b, -1),
        )[kind]()

    for u in range(4):
        gather_copy(u, 0).start()
        gather_copy(u, 1).start()
    for u in range(4):
        gather_copy(u, 0).wait_recv()
        gather_copy(u, 2).start()
        gather_copy(u, 1).wait_recv()
        gather_copy(u, 3).start()
    for u in range(4):
        gather_copy(u, 2).wait_recv()
        gather_copy(u, 3).wait_recv()
        gather_copy(u, 4).start()
        gather_copy(u, 5).start()
    for u in range(4):
        gather_copy(u, 4).wait_recv()
        gather_copy(u, 6).start()
        gather_copy(u, 5).wait_recv()
        gather_copy(u, 7).start()

    table.wait()
    scales.wait()
    scale_row = lvlv[pl.ds(lv[0], 1), :]
    for i in range(samples):
        cond[pl.ds(i, 1), :] = embv[pl.ds(ts[i], 1), :] * scale_row

    @pl.when(seg == 0)
    def _():
        tok_in.wait()

    @pl.when(seg == SECTIONS - 1)
    def _():
        go_in.wait()

    for u in range(4):
        gather_copy(u, 6).wait_recv()
        gather_copy(u, 7).wait_recv()

    def pcopy(kind, m, src, dst, to):
        k = kind * BLOCKS + m
        part = pl.ds(pl.multiple_of(m * step, step), step)
        return pltpu.make_async_remote_copy(
            src_ref=src.at[part, :], dst_ref=dst.at[part, :],
            send_sem=psend.at[k], recv_sem=precv.at[k], device_id={"segment": to},
        )

    def y_next(m):
        return pcopy(0, m, yb, xr, lax.rem(seg + 1, SECTIONS))

    def y_skip(m):
        return pcopy(1, m, yb, sk, SECTIONS - 1 - seg)

    def g_next(m):
        return pcopy(2, m, dx, gr, lax.rem(seg + SECTIONS - 1, SECTIONS))

    def g_skip(m):
        return pcopy(3, m, dx, gk, SECTIONS - 1 - seg)

    def forward(m, carry):
        part = pl.ds(pl.multiple_of(m * step, step), step)

        @pl.when(seg > 0)
        def _():
            y_next(m).wait_recv()

        @pl.when(seg > 4)
        def _():
            y_skip(m).wait_recv()
            xr[part, :] = (xr[part, :].astype(F32) + sk[part, :].astype(F32)).astype(BF)

        row = cond[pl.ds(m // (BLOCKS // samples), 1), :]
        u = xr[part, :].astype(F32) + row
        r = lax.rsqrt(jnp.mean(u * u, axis=-1, keepdims=True) + EPS)
        un[part, :] = u * r
        rr[part, :] = jnp.broadcast_to(r, (step, 128))
        n = (u * r).astype(BF)
        nb[part, :] = n
        for j in range(0, chan, 256):
            cols = pl.ds(j, 256)
            v = dot(n, W1[:, :, :, cols].reshape(chan, 256), ((1,), (0,)))
            s = jax.nn.sigmoid(v)
            hb[part, cols] = (v * s).astype(BF)
            sl[part, cols] = s * (1.0 + v * (1.0 - s))
        h = hb[part, :]
        for j in range(0, chan, 256):
            cols = pl.ds(j, 256)
            v = dot(h, W2[:, :, :, cols].reshape(chan, 256), ((1,), (0,)))
            yb[part, cols] = (xr[part, cols].astype(F32) + v).astype(BF)

        @pl.when(seg < SECTIONS - 1)
        def _():
            y_next(m).start()

        @pl.when(seg < 3)
        def _():
            y_skip(m).start()

        return carry

    lax.fori_loop(0, BLOCKS, forward, 0)

    def turn():
        nT[...] = nb[...].T.reshape(nT.shape)
        hT[...] = hb[...].T.reshape(hT.shape)

    @pl.when(seg < 6)
    def _():
        turn()

    def backward(m, carry):
        part = pl.ds(pl.multiple_of(m * step, step), step)

        @pl.when(seg < SECTIONS - 1)
        def _():
            g_next(m).wait_recv()

        @pl.when(seg < 3)
        def _():
            g_skip(m).wait_recv()
            gr[part, :] = (gr[part, :].astype(F32) + gk[part, :].astype(F32)).astype(BF)

        g = gr[part, :]
        for j in range(2):
            cols = pl.ds(640 * j, 640)
            v = dot(g, W2[2 * j : 2 * j + 2].reshape(640, chan), ((1,), (1,)))
            dz[part, cols] = (v * sl[part, cols]).astype(BF)
        d = dz[part, :]
        for j in range(2):
            cols = pl.ds(640 * j, 640)
            dn[:, cols] = dot(d, W1[2 * j : 2 * j + 2].reshape(640, chan), ((1,), (1,)))
        nrm = un[part, :]
        v = dn[...]
        along = jnp.mean(nrm * v, axis=-1, keepdims=True)
        r = rr[part, pl.ds(0, 1)]
        dx[part, :] = (g.astype(F32) + r * (v - nrm * along)).astype(BF)

        @pl.when(seg > 0)
        def _():
            g_next(m).start()

        @pl.when(seg > 4)
        def _():
            g_skip(m).start()

        return carry

    lax.fori_loop(0, BLOCKS, backward, 0)

    dx_out = pltpu.make_async_copy(dx, dxo.at[0], lsem.at[6])
    dx_out.start()

    @pl.when(seg >= 6)
    def _():
        turn()

    sunits = [(w, h) for w in (1, 0) for h in range(2)]

    def big(h, second, part):
        return (second, part) if h == 0 else (part, second)

    def product(u, second):
        w, h = sunits[u]
        left, right, to = ((nT, dz, G1), (hT, gr, G2))[w]
        i = big(h, second, slice(None))
        v = dot(left[i[0], i[1]].reshape(320, rows), right[:, pl.ds(*HALVES[h])], ((1,), (0,)))
        to[i[0], i[1], :, pl.ds(*HALVES[h])] = v.astype(BF).reshape(4, 80, 640)

    def scopy(u, kind, src, dst, axis, way):
        k = u * 8 + kind
        return pltpu.make_async_remote_copy(
            src_ref=src, dst_ref=dst, send_sem=ssend.at[k], recv_sem=srecv.at[k],
            device_id=dev(axis, way),
        )

    def scatter_copy(u, kind):
        w, h = sunits[u]
        ref = (G1, G2)[w]
        a, b = axes[h]
        pa, pb = offs[a], offs[b]
        return (
            lambda: scopy(u, 0, many(ref, h, pb(2), SUB0), r1.at[u, 0], b, 1),
            lambda: scopy(u, 1, many(ref, h, pb(2), SUB1), r1.at[u, 1], b, -1),
            lambda: scopy(u, 2, many(ref, h, pb(1), SUB), r2.at[u, 0], b, 1),
            lambda: scopy(u, 3, many(ref, h, pb(-1), SUB), r2.at[u, 1], b, -1),
            lambda: scopy(u, 4, one(ref, h, pa(2), pb(0), TOP), r4.at[u, pl.ds(0, 48)], a, 1),
            lambda: scopy(u, 5, one(ref, h, pa(2), pb(0), LOW), r4.at[u, pl.ds(48, 32)], a, -1),
            lambda: scopy(u, 6, one(ref, h, pa(1), pb(0), ALL), r5.at[u, 0], a, 1),
            lambda: scopy(u, 7, one(ref, h, pa(-1), pb(0), ALL), r5.at[u, 1], a, -1),
        )[kind]()

    def add(ref, *values):
        total = ref[...].astype(F32)
        for value in values:
            total = total + value.astype(F32)
        ref[...] = total.astype(BF)

    def parts(u):
        w, h = sunits[u]
        a, b = axes[h]
        return (G1, G2)[w], h, offs[a], offs[b]

    for u in range(4):
        ref, h, pa, pb = parts(u)
        product(u, pb(2))
        scatter_copy(u, 0).start()
        scatter_copy(u, 1).start()
    for u in range(4):
        ref, h, pa, pb = parts(u)
        product(u, pb(1))
        product(u, pb(-1))
        scatter_copy(u, 0).wait_recv()
        add(many(ref, h, pb(1), SUB0), r1[u, 0])
        scatter_copy(u, 2).start()
        scatter_copy(u, 1).wait_recv()
        add(many(ref, h, pb(-1), SUB1), r1[u, 1])
        scatter_copy(u, 3).start()
    for u in range(4):
        ref, h, pa, pb = parts(u)
        product(u, pb(0))
    for u in range(4):
        ref, h, pa, pb = parts(u)
        scatter_copy(u, 2).wait_recv()
        scatter_copy(u, 3).wait_recv()
        add(many(ref, h, pb(0), SUB), r2[u, 0], r2[u, 1])
        scatter_copy(u, 4).start()
        scatter_copy(u, 5).start()
    for u in range(4):
        ref, h, pa, pb = parts(u)
        scatter_copy(u, 4).wait_recv()
        add(one(ref, h, pa(1), pb(0), TOP), r4[u, pl.ds(0, 48)])
        scatter_copy(u, 6).start()
        scatter_copy(u, 5).wait_recv()
        add(one(ref, h, pa(-1), pb(0), LOW), r4[u, pl.ds(48, 32)])
        scatter_copy(u, 7).start()
    for u in range(4):
        w, h = sunits[u]
        ref, h, pa, pb = parts(u)
        scatter_copy(u, 6).wait_recv()
        scatter_copy(u, 7).wait_recv()
        total = one(ref, h, pa(0), pb(0), ALL)[...].astype(F32)
        total = total + r5[u, 0].astype(F32) + r5[u, 1].astype(F32)
        (acc1, acc2)[w][:, pl.ds(*HALVES[h])] = total
    out1 = pltpu.make_async_copy(acc1, fg.at[0], lsem.at[7])
    out2 = pltpu.make_async_copy(acc2, sg.at[0], lsem.at[8])
    out1.start()
    out2.start()

    for u in range(4):
        for kind in range(8):
            gather_copy(u, kind).wait_send()
            scatter_copy(u, kind).wait_send()

    def sent(m, carry):
        @pl.when(seg < SECTIONS - 1)
        def _():
            y_next(m).wait_send()

        @pl.when(seg < 3)
        def _():
            y_skip(m).wait_send()

        @pl.when(seg > 0)
        def _():
            g_next(m).wait_send()

        @pl.when(seg > 4)
        def _():
            g_skip(m).wait_send()

        return carry

    lax.fori_loop(0, BLOCKS, sent, 0)
    dx_out.wait()
    out1.wait()
    out2.wait()


def local(tokens, grad_out, first_weight, second_weight, emb_table, level_scale, timesteps, levels):
    rows, chan = tokens.shape
    depth = first_weight.shape[1]
    step = rows // BLOCKS
    samples = timesteps.shape[0]
    full = (RING, RING, depth, chan)
    vm = pltpu.VMEM
    dma = pltpu.SemaphoreType.DMA
    act = vm((rows, chan), BF)
    act32 = vm((rows, chan), F32)
    anyspec = pl.BlockSpec(memory_space=pl.ANY)
    smem = pl.BlockSpec(memory_space=pltpu.SMEM)
    macs = 6 * rows * chan * chan
    return pl.pallas_call(
        kernel,
        out_shape=(
            jax.ShapeDtypeStruct((1, depth, chan), F32),
            jax.ShapeDtypeStruct((1, depth, chan), F32),
            jax.ShapeDtypeStruct((1, rows, chan), BF),
        ),
        in_specs=[anyspec] * 6 + [smem] * 2,
        out_specs=(anyspec,) * 3,
        scratch_shapes=[
            vm(full, BF), vm(full, BF), vm(full, BF), vm(full, BF),
            vm((RING, RING, depth, rows), BF), vm((RING, RING, depth, rows), BF),
            act, act, act, act, act, act32, act32, act, act, act,
            vm((step, chan), F32), act, vm((rows, 128), F32), vm((samples, chan), F32),
            vm(emb_table.shape, F32), vm(level_scale.shape, F32),
            vm((depth, chan), F32), vm((depth, chan), F32),
            vm((4, 2, 2, depth, 640), BF), vm((4, 2, 4, depth, 640), BF),
            vm((4, depth, 640), BF), vm((4, 2, depth, 640), BF),
            dma((32,)), dma((32,)), dma((32,)), dma((32,)),
            dma((4 * BLOCKS,)), dma((4 * BLOCKS,)), dma((9,)),
        ],
        compiler_params=pltpu.CompilerParams(
            collective_id=0, has_side_effects=True, vmem_limit_bytes=60 * 1024 * 1024
        ),
        cost_estimate=pl.CostEstimate(
            flops=2 * macs, bytes_accessed=16 * 1024 * 1024, transcendentals=rows * chan
        ),
        name="sections",
    )(tokens, grad_out, first_weight, second_weight, emb_table, level_scale, timesteps, levels)


def solution(mesh):
    weights = P("segment", "dp", None)
    in_specs = (P("dp", None), P("dp", None), weights, weights, P(), P(), P("dp"), P("segment"))
    out_specs = (weights, weights, weights)
    return jax.shard_map(local, mesh=mesh, in_specs=in_specs, out_specs=out_specs, check_vma=False)
```

time: 662 us -> 172 us (0.26)
  waiting for transfers between devices: 355 us -> 0 us
  starting transfers between devices: 195 us -> 0 us
  Pallas kernels: 0 us -> 165 us
  local copies, waits for them, and re-layouts: 57 us -> 5.52 us
  matrix products: 22.8 us -> 0 us
  other arithmetic: 16 us -> 0 us
  between operations: 14.5 us -> 1.29 us
    ppermute x22 -> x0, starting transfers between devices: 195 us -> none  [the longest x6 100 us: partner(): return lax.ppermute(block, axis, route)]
    ppermute x22 -> x0, waiting for transfers between devices: 176 us -> none  [the longest x16 110 us: shifted(): lax.ppermute(value, axis, [(source, source + steps) for source in range(l...]
    pallas_call x0 -> x1, Pallas kernels: none -> 165 us  [local(): pl.pallas_call(kernel, out_shape=(jax.ShapeDtypeStruct((1, depth, chan),...]
    all_gather x2 -> x0, waiting for transfers between devices: 96.8 us -> none  [the longest x1 49.4 us: local(): lax.all_gather(second_weight, 'dp', axis=1, tiled=True)]
    unnamed x4 -> x0, waiting for transfers between devices: 82.6 us -> none
    dot_general x8 -> x0, matrix products: 22.8 us -> none  [the longest x2 7 us: times_transpose(): lax.dot_general(left, right, (((1,), (1,)), ((), ())), preferred_element_...]
    another operation x23 -> x0, local copies, waits for them, and re-layouts: 20.7 us -> none
    broadcast_in_dim x18 -> x0, local copies, waits for them, and re-layouts: 19.6 us -> none  [the longest x16 18.4 us: local(): jnp.repeat(sample_rows * level_row, row_count // timesteps.shape[0], axis=0)]
  transfers between devices with their start and end apart: 25 -> 0, of which waited for: 25 -> 0; matrix products, arithmetic and copies ran while one was open for 1% -> 0% of each run, Pallas kernels for 0% -> 0%
where the time goes in v1:
time: 172 us; the launch traced here: 171 us
  Pallas kernels  165 us (96%)
  local copies, waits for them, and re-layouts  5.52 us (3%)
    pallas_call x1, Pallas kernels, local(): pl.pallas_call(kernel, out_shape=(jax.ShapeDtypeStruct((1, depth, chan),...  165 us
    unnamed x3, local copies, waits for them, and re-layouts  5.52 us

profile of v1, /device:TPU:0, one launch (start us, length us, event | category | flops | bytes accessed | tf_op | source)
XLA Modules:
  0.0 171.4 jit_solution(16571614485541049616)
XLA Ops:
  1.3 164.6 %sections.1 = (f32[1,80,1280]{2,1,0:T(8,128)}, f32[1,80,1280]{2,1,0:T(8,128)}, bf16[1,256,1280]{2,1,0:T(8,128)(2,1)}) custom-call(bf16[256,1280]{1,0:T(8,128)(2,1)} %tok.1, bf16[256,1280]{1,0:T(8,128)(2,1)} %go.1, bf16[1,80,1280]{2,1,0:T(8,128)(2,1)} %w1.1, bf16[1,80,1280]{2,1,0:T(8,128)(2,1)} %w2.1, f32[1000,1280]{1,0:T(8,128)} %emb.1, f32[4,1280]{1,0:T(4,128)} %lvl.1, ...), custom_call_target="tpu_custom_call" | custom-call | flops 5033164800 | bytes 16777216 | tf_op jit(solution)/shard_map/sections/pallas_call | solution.py:423
  165.9 1.8 %copy.15 = f32[1,80,1280]{2,1,0:T(8,128)} copy(f32[1,80,1280]{2,1,0:T(8,128)} %get-tuple-element.6) | data formatting | bytes 819200
  167.6 1.8 %copy.16 = f32[1,80,1280]{2,1,0:T(8,128)} copy(f32[1,80,1280]{2,1,0:T(8,128)} %get-tuple-element.7) | data formatting | bytes 819200
  169.4 2.0 %copy.17 = bf16[1,256,1280]{2,1,0:T(8,128)(2,1)} copy(bf16[1,256,1280]{2,1,0:T(8,128)(2,1)} %get-tuple-element.8) | data formatting | bytes 1310720

commit v2 on v1

v2 whole, which is shorter than its diff:
```python
import functools

import jax
import jax.numpy as jnp
from jax import lax
from jax.experimental import pallas as pl
from jax.experimental.pallas import tpu as pltpu
from jax.sharding import PartitionSpec as P

EPS = 1e-06
SECTIONS = 8
RING = 4
BLOCKS = 4
HALVES = ((0, 640), (640, 640))
F32 = jnp.float32
BF = jnp.bfloat16


def dot(a, b, contract):
    return lax.dot_general(a, b, (contract, ((), ())), preferred_element_type=F32)


def kernel(
    tok, go, w1, w2, emb, lvl, ts, lv,
    fg, sg, dxo,
    W1, W2, T1, T2, G1, G2, nT, hT,
    xr, sk, yb, nb, hb, un, sl, gr, gk, dz, dn, dx, rr, cond,
    embv, lvlv, acc1, acc2, r1, r2, r4, r5,
    gsend, grecv, ssend, srecv, psend, precv, lsem,
):
    seg = lax.axis_index("segment")
    dp = lax.axis_index("dp")
    z, x = dp // RING, dp % RING
    rows, chan = xr.shape
    step = rows // BLOCKS
    samples = ts.shape[0]

    def at_z(i):
        return lax.rem(z + i + RING, RING)

    def at_x(i):
        return lax.rem(x + i + RING, RING)

    def dev(axis, i):
        return {"dp": at_z(i) * RING + x} if axis == "z" else {"dp": z * RING + at_x(i)}

    own1 = pltpu.make_async_copy(w1.at[0], W1.at[z, x], lsem.at[0])
    own2 = pltpu.make_async_copy(w2.at[0], W2.at[z, x], lsem.at[1])
    table = pltpu.make_async_copy(emb, embv, lsem.at[2])
    scales = pltpu.make_async_copy(lvl, lvlv, lsem.at[3])
    own1.start()
    own2.start()
    table.start()
    scales.start()
    tok_in = pltpu.make_async_copy(tok, xr, lsem.at[4])
    go_in = pltpu.make_async_copy(go, gr, lsem.at[5])

    @pl.when(seg == 0)
    def _():
        tok_in.start()

    @pl.when(seg == SECTIONS - 1)
    def _():
        go_in.start()

    barrier = pltpu.get_barrier_semaphore()
    for axis in ("z", "x"):
        for way in (1, -1):
            pl.semaphore_signal(barrier, inc=1, device_id=dev(axis, way))

    @pl.when(seg > 0)
    def _():
        pl.semaphore_signal(barrier, inc=1, device_id={"segment": seg - 1})

    @pl.when(seg < SECTIONS - 1)
    def _():
        pl.semaphore_signal(barrier, inc=1, device_id={"segment": seg + 1})

    relay = jnp.logical_and(seg > 1, seg < 6)

    @pl.when(relay)
    def _():
        pl.semaphore_signal(barrier, inc=1, device_id={"segment": jnp.where(seg < 4, seg + 2, seg - 2)})

    far = jnp.logical_or(seg < 3, seg > 4)

    @pl.when(far)
    def _():
        pl.semaphore_signal(barrier, inc=1, device_id={"segment": SECTIONS - 1 - seg})

    pl.semaphore_wait(
        barrier,
        4
        + (seg > 0).astype(jnp.int32)
        + (seg < SECTIONS - 1).astype(jnp.int32)
        + far.astype(jnp.int32)
        + relay.astype(jnp.int32),
    )
    own1.wait()
    own2.wait()

    units = [(w, h) for w in range(2) for h in range(2)]
    axes = (("x", "z"), ("z", "x"))
    offs = {"x": at_x, "z": at_z}
    ALL, TOP, LOW = pl.ds(0, 80), pl.ds(0, 48), pl.ds(48, 32)

    def one(ref, h, first, second, part=ALL):
        i = (second, first) if h == 0 else (first, second)
        return ref.at[i[0], i[1], part, pl.ds(*HALVES[h])]

    def gcopy(u, kind, first, second, part, leg, way):
        w, h = units[u]
        ref = one((W1, W2)[w], h, offs[axes[h][0]](first), offs[axes[h][1]](second), part)
        k = u * 16 + kind
        return pltpu.make_async_remote_copy(
            src_ref=ref, dst_ref=ref, send_sem=gsend.at[k], recv_sem=grecv.at[k],
            device_id=dev(axes[h][leg], way),
        )

    NEAR = (0, -1, 1, 2)

    def first_leg(u, kind):
        return gcopy(
            u, kind, (0, 0, -1, 1)[kind], 0, (ALL, ALL, TOP, LOW)[kind], 0, (1, -1, 1, -1)[kind]
        )

    def second_leg(u, i, way):
        return gcopy(u, 4 + 2 * i + (way < 0), NEAR[i], 0, ALL, 1, way)

    def second_on(u, i):
        way = 1 if i < 2 else -1
        return gcopy(u, 12 + i, NEAR[i], -way, ALL, 1, way)

    def spread(u, i):
        second_leg(u, i, 1).start()
        second_leg(u, i, -1).start()

    def pass_on(u, i):
        second_leg(u, i, 1 if i < 2 else -1).wait_recv()
        second_on(u, i).start()

    for u in range(4):
        first_leg(u, 0).start()
        first_leg(u, 1).start()
    for u in range(4):
        spread(u, 0)
    for u in range(4):
        first_leg(u, 0).wait_recv()
        first_leg(u, 2).start()
        first_leg(u, 1).wait_recv()
        first_leg(u, 3).start()
        spread(u, 1)
        spread(u, 2)
    for u in range(4):
        pass_on(u, 0)
        first_leg(u, 2).wait_recv()
        first_leg(u, 3).wait_recv()
        spread(u, 3)
    for i in range(1, 4):
        for u in range(4):
            pass_on(u, i)

    table.wait()
    scales.wait()
    scale_row = lvlv[pl.ds(lv[0], 1), :]
    for i in range(samples):
        cond[pl.ds(i, 1), :] = embv[pl.ds(ts[i], 1), :] * scale_row

    @pl.when(seg == 0)
    def _():
        tok_in.wait()

    @pl.when(seg == SECTIONS - 1)
    def _():
        go_in.wait()

    for u in range(4):
        for i in range(4):
            second_leg(u, i, -1 if i < 2 else 1).wait_recv()
            second_on(u, i).wait_recv()

    def transpose_weights():
        for j in range(0, chan, 256):
            T1[pl.ds(j, 256), :] = W1[:, :, :, pl.ds(j, 256)].reshape(chan, 256).T
            T2[pl.ds(j, 256), :] = W2[:, :, :, pl.ds(j, 256)].reshape(chan, 256).T

    @pl.when(seg >= 4)
    def _():
        transpose_weights()

    def pcopy(kind, m, src, dst, to):
        k = kind * BLOCKS + m
        part = pl.ds(pl.multiple_of(m * step, step), step)
        return pltpu.make_async_remote_copy(
            src_ref=src.at[part, :], dst_ref=dst.at[part, :],
            send_sem=psend.at[k], recv_sem=precv.at[k], device_id={"segment": to},
        )

    def y_next(m):
        return pcopy(0, m, yb, xr, lax.rem(seg + 1, SECTIONS))

    def y_skip(m):
        return pcopy(1, m, yb, sk, SECTIONS - 1 - seg)

    def g_next(m):
        return pcopy(2, m, dx, gr, lax.rem(seg + SECTIONS - 1, SECTIONS))

    def g_skip(m):
        return pcopy(3, m, dx, gk, SECTIONS - 1 - seg)

    def y_relay(m):
        return pcopy(1, m, xr, sk, lax.rem(seg + 2, SECTIONS))

    def g_relay(m):
        return pcopy(3, m, gr, gk, lax.rem(seg + SECTIONS - 2, SECTIONS))

    early = BLOCKS // 2

    def y_direct(m):
        return jnp.logical_or(seg < 2, jnp.logical_and(seg == 2, m < early))

    def g_direct(m):
        return jnp.logical_or(seg > 5, jnp.logical_and(seg == 5, m < early))

    def forward(m, carry):
        part = pl.ds(pl.multiple_of(m * step, step), step)

        @pl.when(seg > 0)
        def _():
            y_next(m).wait_recv()

        @pl.when(seg > 4)
        def _():
            y_skip(m).wait_recv()
            xr[part, :] = (xr[part, :].astype(F32) + sk[part, :].astype(F32)).astype(BF)

        row = cond[pl.ds(m // (BLOCKS // samples), 1), :]
        u = xr[part, :].astype(F32) + row
        r = lax.rsqrt(jnp.mean(u * u, axis=-1, keepdims=True) + EPS)
        un[part, :] = u * r
        rr[part, :] = jnp.broadcast_to(r, (step, 128))
        n = (u * r).astype(BF)
        nb[part, :] = n
        for j in range(0, chan, 256):
            cols = pl.ds(j, 256)
            v = dot(n, W1[:, :, :, cols].reshape(chan, 256), ((1,), (0,)))
            s = jax.nn.sigmoid(v)
            hb[part, cols] = (v * s).astype(BF)
            sl[part, cols] = s * (1.0 + v * (1.0 - s))
        h = hb[part, :]
        for j in range(0, chan, 256):
            cols = pl.ds(j, 256)
            v = dot(h, W2[:, :, :, cols].reshape(chan, 256), ((1,), (0,)))
            yb[part, cols] = (xr[part, cols].astype(F32) + v).astype(BF)

        @pl.when(seg < SECTIONS - 1)
        def _():
            y_next(m).start()

        @pl.when(y_direct(m))
        def _():
            y_skip(m).start()

        return carry

    lax.fori_loop(0, BLOCKS, forward, 0)

    @pl.when(seg == 3)
    def _():
        for m in range(early, BLOCKS):
            y_relay(m).start()

    @pl.when(seg < 4)
    def _():
        transpose_weights()

    def turn():
        nT[...] = nb[...].T.reshape(nT.shape)
        hT[...] = hb[...].T.reshape(hT.shape)

    @pl.when(seg < 6)
    def _():
        turn()

    def backward(m, carry):
        part = pl.ds(pl.multiple_of(m * step, step), step)

        @pl.when(seg < SECTIONS - 1)
        def _():
            g_next(m).wait_recv()

        @pl.when(seg < 3)
        def _():
            g_skip(m).wait_recv()
            gr[part, :] = (gr[part, :].astype(F32) + gk[part, :].astype(F32)).astype(BF)

        g = gr[part, :]
        for j in range(0, chan, 256):
            cols = pl.ds(j, 256)
            v = dot(g, T2[:, cols], ((1,), (0,)))
            dz[part, cols] = (v * sl[part, cols]).astype(BF)
        d = dz[part, :]
        for j in range(0, chan, 256):
            cols = pl.ds(j, 256)
            dn[:, cols] = dot(d, T1[:, cols], ((1,), (0,)))
        nrm = un[part, :]
        v = dn[...]
        along = jnp.mean(nrm * v, axis=-1, keepdims=True)
        r = rr[part, pl.ds(0, 1)]
        dx[part, :] = (g.astype(F32) + r * (v - nrm * along)).astype(BF)

        @pl.when(seg > 0)
        def _():
            g_next(m).start()

        @pl.when(g_direct(m))
        def _():
            g_skip(m).start()

        return carry

    lax.fori_loop(0, BLOCKS, backward, 0)

    @pl.when(seg == 4)
    def _():
        for m in range(early, BLOCKS):
            g_relay(m).start()

    dx_out = pltpu.make_async_copy(dx, dxo.at[0], lsem.at[6])
    dx_out.start()

    @pl.when(seg >= 6)
    def _():
        turn()

    sunits = [(w, h) for w in (1, 0) for h in range(2)]
    FAR = (2, 1, -1, 0)

    def product(u, i):
        w, h = sunits[u]
        left, right, to = ((nT, dz, G1), (hT, gr, G2))[w]
        at = offs[axes[h][0]](FAR[i])
        at = (slice(None), at) if h == 0 else (at, slice(None))
        v = dot(left[at[0], at[1]].reshape(320, rows), right[:, pl.ds(*HALVES[h])], ((1,), (0,)))
        to[at[0], at[1], :, pl.ds(*HALVES[h])] = v.astype(BF).reshape(4, 80, 640)

    def block(u, first, second, part=ALL):
        w, h = sunits[u]
        return one((G1, G2)[w], h, offs[axes[h][0]](first), offs[axes[h][1]](second), part)

    def scopy(u, kind, src, dst, leg, way):
        k = u * 16 + kind
        return pltpu.make_async_remote_copy(
            src_ref=src, dst_ref=dst, send_sem=ssend.at[k], recv_sem=srecv.at[k],
            device_id=dev(axes[sunits[u][1]][leg], way),
        )

    def out_way(i):
        return 1 if i < 2 else -1

    def opposite(u, i):
        return scopy(u, i, block(u, FAR[i], 2), r1.at[u, i], 1, out_way(i))

    def beside(u, i, way):
        k = 4 + 2 * i + (way < 0)
        return scopy(u, k, block(u, FAR[i], way), r2.at[u, i, int(way < 0)], 1, way)

    def last_opposite(u, way):
        part = TOP if way > 0 else LOW
        return scopy(u, 12 + (way < 0), block(u, 2, 0, part), r4.at[u, part], 0, way)

    def last_beside(u, way):
        return scopy(u, 14 + (way < 0), block(u, way, 0), r5.at[u, int(way < 0)], 0, way)

    def add(ref, *values):
        total = ref[...].astype(F32)
        for value in values:
            total = total + value.astype(F32)
        ref[...] = total.astype(BF)

    def leave(u, i):
        product(u, i)
        opposite(u, i).start()

    def go_beside(u, i):
        way = out_way(i)
        beside(u, i, -way).start()
        opposite(u, i).wait_recv()
        add(block(u, FAR[i], way), r1[u, i])
        beside(u, i, way).start()

    def arrive(u, i):
        beside(u, i, 1).wait_recv()
        beside(u, i, -1).wait_recv()
        if i < 3:
            add(block(u, FAR[i], 0), r2[u, i, 0], r2[u, i, 1])
        if i == 0:
            last_opposite(u, 1).start()
            last_opposite(u, -1).start()
        elif i < 3:
            way = FAR[i]
            part = TOP if way > 0 else LOW
            last_opposite(u, way).wait_recv()
            add(block(u, way, 0, part), r4[u, part])
            last_beside(u, way).start()
        else:
            last_beside(u, 1).wait_recv()
            last_beside(u, -1).wait_recv()
            w, h = sunits[u]
            total = block(u, 0, 0)[...].astype(F32)
            for value in (r2[u, i, 0], r2[u, i, 1], r5[u, 0], r5[u, 1]):
                total = total + value.astype(F32)
            (acc1, acc2)[w][:, pl.ds(*HALVES[h])] = total

    for i in range(6):
        if i < 4:
            for u in range(4):
                leave(u, i)
        if 1 <= i < 5:
            for u in range(4):
                go_beside(u, i - 1)
        if 2 <= i:
            for u in range(4):
                arrive(u, i - 2)
    out1 = pltpu.make_async_copy(acc1, fg.at[0], lsem.at[7])
    out2 = pltpu.make_async_copy(acc2, sg.at[0], lsem.at[8])
    out1.start()
    out2.start()

    for u in range(4):
        for k in range(4):
            first_leg(u, k).wait_send()
            second_leg(u, k, 1).wait_send()
            second_leg(u, k, -1).wait_send()
            second_on(u, k).wait_send()
            opposite(u, k).wait_send()
            beside(u, k, 1).wait_send()
            beside(u, k, -1).wait_send()
        for way in (1, -1):
            last_opposite(u, way).wait_send()
            last_beside(u, way).wait_send()

    @pl.when(seg == 3)
    def _():
        for m in range(early, BLOCKS):
            y_relay(m).wait_send()

    @pl.when(seg == 4)
    def _():
        for m in range(early, BLOCKS):
            g_relay(m).wait_send()

    def sent(m, carry):
        @pl.when(seg < SECTIONS - 1)
        def _():
            y_next(m).wait_send()

        @pl.when(y_direct(m))
        def _():
            y_skip(m).wait_send()

        @pl.when(seg > 0)
        def _():
            g_next(m).wait_send()

        @pl.when(g_direct(m))
        def _():
            g_skip(m).wait_send()

        return carry

    lax.fori_loop(0, BLOCKS, sent, 0)
    dx_out.wait()
    out1.wait()
    out2.wait()


def local(tokens, grad_out, first_weight, second_weight, emb_table, level_scale, timesteps, levels):
    rows, chan = tokens.shape
    depth = first_weight.shape[1]
    step = rows // BLOCKS
    samples = timesteps.shape[0]
    full = (RING, RING, depth, chan)
    vm = pltpu.VMEM
    dma = pltpu.SemaphoreType.DMA
    act = vm((rows, chan), BF)
    act32 = vm((rows, chan), F32)
    anyspec = pl.BlockSpec(memory_space=pl.ANY)
    smem = pl.BlockSpec(memory_space=pltpu.SMEM)
    macs = 6 * rows * chan * chan
    return pl.pallas_call(
        kernel,
        out_shape=(
            jax.ShapeDtypeStruct((1, depth, chan), F32),
            jax.ShapeDtypeStruct((1, depth, chan), F32),
            jax.ShapeDtypeStruct((1, rows, chan), BF),
        ),
        in_specs=[anyspec] * 6 + [smem] * 2,
        out_specs=(anyspec,) * 3,
        scratch_shapes=[
            vm(full, BF), vm(full, BF), vm((chan, chan), BF), vm((chan, chan), BF),
            vm(full, BF), vm(full, BF),
            vm((RING, RING, depth, rows), BF), vm((RING, RING, depth, rows), BF),
            act, act, act, act, act, act32, act32, act, act, act,
            vm((step, chan), F32), act, vm((rows, 128), F32), vm((samples, chan), F32),
            vm(emb_table.shape, F32), vm(level_scale.shape, F32),
            vm((depth, chan), F32), vm((depth, chan), F32),
            vm((4, 4, depth, 640), BF), vm((4, 4, 2, depth, 640), BF),
            vm((4, depth, 640), BF), vm((4, 2, depth, 640), BF),
            dma((64,)), dma((64,)), dma((64,)), dma((64,)),
            dma((4 * BLOCKS,)), dma((4 * BLOCKS,)), dma((9,)),
        ],
        compiler_params=pltpu.CompilerParams(
            collective_id=0, has_side_effects=True, vmem_limit_bytes=60 * 1024 * 1024
        ),
        cost_estimate=pl.CostEstimate(
            flops=2 * macs, bytes_accessed=16 * 1024 * 1024, transcendentals=rows * chan
        ),
        name="sections",
    )(tokens, grad_out, first_weight, second_weight, emb_table, level_scale, timesteps, levels)


def solution(mesh):
    weights = P("segment", "dp", None)
    in_specs = (P("dp", None), P("dp", None), weights, weights, P(), P(), P("dp"), P("segment"))
    out_specs = (weights, weights, weights)
    return jax.shard_map(local, mesh=mesh, in_specs=in_specs, out_specs=out_specs, check_vma=False)
```

time: 172 us -> 159 us (0.924)
  Pallas kernels: 165 us -> 151 us
    pallas_call x1, Pallas kernels: 165 us -> 151 us  [local(): pl.pallas_call(kernel, out_shape=(jax.ShapeDtypeStruct((1, depth, chan),...]
where the time goes in v2:
time: 159 us; the launch traced here: 158 us
  Pallas kernels  151 us (95%)
  local copies, waits for them, and re-layouts  5.52 us (3%)
    pallas_call x1, Pallas kernels, local(): pl.pallas_call(kernel, out_shape=(jax.ShapeDtypeStruct((1, depth, chan),...  151 us
    unnamed x3, local copies, waits for them, and re-layouts  5.52 us

profile of v2, /device:TPU:0, one launch (start us, length us, event | category | flops | bytes accessed | tf_op | source)
XLA Modules:
  0.0 157.8 jit_solution(14769669556686399771)
XLA Ops:
  1.3 151.0 %sections.1 = (f32[1,80,1280]{2,1,0:T(8,128)}, f32[1,80,1280]{2,1,0:T(8,128)}, bf16[1,256,1280]{2,1,0:T(8,128)(2,1)}) custom-call(bf16[256,1280]{1,0:T(8,128)(2,1)} %tok.1, bf16[256,1280]{1,0:T(8,128)(2,1)} %go.1, bf16[1,80,1280]{2,1,0:T(8,128)(2,1)} %w1.1, bf16[1,80,1280]{2,1,0:T(8,128)(2,1)} %w2.1, f32[1000,1280]{1,0:T(8,128)} %emb.1, f32[4,1280]{1,0:T(4,128)} %lvl.1, ...), custom_call_target="tpu_custom_call" | custom-call | flops 5033164800 | bytes 16777216 | tf_op jit(solution)/shard_map/sections/pallas_call | solution.py:491
  152.3 1.8 %copy.15 = f32[1,80,1280]{2,1,0:T(8,128)} copy(f32[1,80,1280]{2,1,0:T(8,128)} %get-tuple-element.6) | data formatting | bytes 819200
  154.0 1.8 %copy.16 = f32[1,80,1280]{2,1,0:T(8,128)} copy(f32[1,80,1280]{2,1,0:T(8,128)} %get-tuple-element.7) | data formatting | bytes 819200
  155.8 2.0 %copy.17 = bf16[1,256,1280]{2,1,0:T(8,128)(2,1)} copy(bf16[1,256,1280]{2,1,0:T(8,128)(2,1)} %get-tuple-element.8) | data formatting | bytes 1310720

commit v3 on v2

--- a/solution.py
+++ b/solution.py
@@ -10,6 +10,7 @@
 EPS = 1e-06
 SECTIONS = 8
 RING = 4
+HELPER = 7
 BLOCKS = 4
 HALVES = ((0, 640), (640, 640))
 F32 = jnp.float32
@@ -25,8 +26,9 @@
     fg, sg, dxo,
     W1, W2, T1, T2, G1, G2, nT, hT,
     xr, sk, yb, nb, hb, un, sl, gr, gk, dz, dn, dx, rr, cond,
+    hz, gz, hU, G3, accb, accr,
     embv, lvlv, acc1, acc2, r1, r2, r4, r5,
-    gsend, grecv, ssend, srecv, psend, precv, lsem,
+    gsend, grecv, ssend, srecv, psend, precv, lsem, turn_sem,
 ):
     seg = lax.axis_index("segment")
     dp = lax.axis_index("dp")
@@ -138,6 +140,12 @@
     def pass_on(u, i):
         second_leg(u, i, 1 if i < 2 else -1).wait_recv()
         second_on(u, i).start()
+
+    odd = lax.rem(seg, 2) == 1
+
+    @pl.when(odd)
+    def _():
+        pl.semaphore_wait(turn_sem, 1)
 
     for u in range(4):
         first_leg(u, 0).start()
@@ -156,6 +164,11 @@
         first_leg(u, 2).wait_recv()
         first_leg(u, 3).wait_recv()
         spread(u, 3)
+
+    @pl.when(jnp.logical_not(odd))
+    def _():
+        pl.semaphore_signal(turn_sem, inc=1, device_id={"segment": lax.rem(seg + 1, SECTIONS)})
+
     for i in range(1, 4):
         for u in range(4):
             pass_on(u, i)
@@ -213,6 +226,12 @@
 
     def g_relay(m):
         return pcopy(3, m, gr, gk, lax.rem(seg + SECTIONS - 2, SECTIONS))
+
+    def h_out(m):
+        return pcopy(4, m, hb, hz, HELPER)
+
+    def g_out(m):
+        return pcopy(5, m, gr, gz, HELPER)
 
     early = BLOCKS // 2
 
@@ -270,6 +289,11 @@
         for m in range(early, BLOCKS):
             y_relay(m).start()
 
+    @pl.when(seg == 0)
+    def _():
+        for m in range(BLOCKS):
+            h_out(m).start()
+
     @pl.when(seg < 4)
     def _():
         transpose_weights()
@@ -293,6 +317,10 @@
         def _():
             g_skip(m).wait_recv()
             gr[part, :] = (gr[part, :].astype(F32) + gk[part, :].astype(F32)).astype(BF)
+
+        @pl.when(seg == 0)
+        def _():
+            g_out(m).start()
 
         g = gr[part, :]
         for j in range(0, chan, 256):
@@ -333,12 +361,12 @@
     def _():
         turn()
 
-    sunits = [(w, h) for w in (1, 0) for h in range(2)]
+    sunits = [(w, h) for w in (1, 0, 2) for h in range(2)]
     FAR = (2, 1, -1, 0)
 
     def product(u, i):
         w, h = sunits[u]
-        left, right, to = ((nT, dz, G1), (hT, gr, G2))[w]
+        left, right, to = ((nT, dz, G1), (hT, gr, G2), (hU, gz, G3))[w]
         at = offs[axes[h][0]](FAR[i])
         at = (slice(None), at) if h == 0 else (at, slice(None))
         v = dot(left[at[0], at[1]].reshape(320, rows), right[:, pl.ds(*HALVES[h])], ((1,), (0,)))
@@ -346,7 +374,7 @@
 
     def block(u, first, second, part=ALL):
         w, h = sunits[u]
-        return one((G1, G2)[w], h, offs[axes[h][0]](first), offs[axes[h][1]](second), part)
+        return one((G1, G2, G3)[w], h, offs[axes[h][0]](first), offs[axes[h][1]](second), part)
 
     def scopy(u, kind, src, dst, leg, way):
         k = u * 16 + kind
@@ -381,10 +409,10 @@
     def leave(u, i):
         product(u, i)
         opposite(u, i).start()
+        beside(u, i, -out_way(i)).start()
 
     def go_beside(u, i):
         way = out_way(i)
-        beside(u, i, -way).start()
         opposite(u, i).wait_recv()
         add(block(u, FAR[i], way), r1[u, i])
         beside(u, i, way).start()
@@ -410,22 +438,77 @@
             total = block(u, 0, 0)[...].astype(F32)
             for value in (r2[u, i, 0], r2[u, i, 1], r5[u, 0], r5[u, 1]):
                 total = total + value.astype(F32)
-            (acc1, acc2)[w][:, pl.ds(*HALVES[h])] = total
-
-    for i in range(6):
-        if i < 4:
-            for u in range(4):
-                leave(u, i)
-        if 1 <= i < 5:
-            for u in range(4):
-                go_beside(u, i - 1)
-        if 2 <= i:
-            for u in range(4):
-                arrive(u, i - 2)
+            to = (acc1, acc2, accb)[w]
+            to[:, pl.ds(*HALVES[h])] = total.astype(to.dtype)
+
+    def ours(u, do):
+        if u < 2:
+            pl.when(seg != 0)(do)
+        else:
+            do()
+
+    def group(units, *steps):
+        for u in units:
+            ours(u, lambda: [step(u, i) for step, i in steps] and None)
+
+    def result(h):
+        part = pl.ds(*HALVES[h])
+        return pltpu.make_async_remote_copy(
+            src_ref=accb.at[:, part], dst_ref=accr.at[:, part],
+            send_sem=ssend.at[96 + h], recv_sem=srecv.at[96 + h],
+            device_id={"segment": lax.rem(seg + SECTIONS - HELPER, SECTIONS)},
+        )
+
+    def helper(do):
+        pl.when(seg == HELPER)(do)
+
+    def take_over():
+        for m in range(BLOCKS):
+            h_out(m).wait_recv()
+            g_out(m).wait_recv()
+        hU[...] = hz[...].T.reshape(hU.shape)
+        group(more, (leave, 0), (leave, 2))
+        group(more, (leave, 1), (leave, 3))
+
+    def give_back():
+        group(more, (go_beside, 1), (go_beside, 3))
+        for i in (2, 1, 3):
+            group(more, (arrive, i))
+        result(0).start()
+        result(1).start()
+
+    own, more = range(4), range(4, 6)
+    group(own, (leave, 0), (leave, 2))
+    group(own, (go_beside, 0), (go_beside, 2))
+    group(own, (leave, 1), (leave, 3))
+    group(own, (arrive, 0))
+    group(own, (go_beside, 1), (go_beside, 3))
+    group(own, (arrive, 2))
+    helper(take_over)
+    group(own, (arrive, 1))
+    helper(lambda: group(more, (go_beside, 0), (go_beside, 2), (arrive, 0)))
+    group(own, (arrive, 3))
+    helper(give_back)
+
+    @pl.when(seg == 0)
+    def _():
+        for h in range(2):
+            result(h).wait_recv()
+        acc2[...] = accr[...].astype(F32)
+
     out1 = pltpu.make_async_copy(acc1, fg.at[0], lsem.at[7])
     out2 = pltpu.make_async_copy(acc2, sg.at[0], lsem.at[8])
     out1.start()
     out2.start()
+
+    def scattered(u):
+        for k in range(4):
+            opposite(u, k).wait_send()
+            beside(u, k, 1).wait_send()
+            beside(u, k, -1).wait_send()
+        for way in (1, -1):
+            last_opposite(u, way).wait_send()
+            last_beside(u, way).wait_send()
 
     for u in range(4):
         for k in range(4):
@@ -433,12 +516,19 @@
             second_leg(u, k, 1).wait_send()
             second_leg(u, k, -1).wait_send()
             second_on(u, k).wait_send()
-            opposite(u, k).wait_send()
-            beside(u, k, 1).wait_send()
-            beside(u, k, -1).wait_send()
-        for way in (1, -1):
-            last_opposite(u, way).wait_send()
-            last_beside(u, way).wait_send()
+        ours(u, lambda: scattered(u))
+
+    @pl.when(seg == HELPER)
+    def _():
+        for h in range(2):
+            scattered(4 + h)
+            result(h).wait_send()
+
+    @pl.when(seg == 0)
+    def _():
+        for m in range(BLOCKS):
+            h_out(m).wait_send()
+            g_out(m).wait_send()
 
     @pl.when(seg == 3)
     def _():
@@ -473,6 +563,12 @@
     dx_out.wait()
     out1.wait()
     out2.wait()
+
+
+def hand_over(a, b, c, out_a, out_b, out_c):
+    out_a[...] = a[...]
+    out_b[...] = b[...]
+    out_c[...] = c[...]
 
 
 def local(tokens, grad_out, first_weight, second_weight, emb_table, level_scale, timesteps, levels):
@@ -486,9 +582,10 @@
     act = vm((rows, chan), BF)
     act32 = vm((rows, chan), F32)
     anyspec = pl.BlockSpec(memory_space=pl.ANY)
+    vmspec = pl.BlockSpec(memory_space=pltpu.VMEM)
     smem = pl.BlockSpec(memory_space=pltpu.SMEM)
     macs = 6 * rows * chan * chan
-    return pl.pallas_call(
+    results = pl.pallas_call(
         kernel,
         out_shape=(
             jax.ShapeDtypeStruct((1, depth, chan), F32),
@@ -503,12 +600,14 @@
             vm((RING, RING, depth, rows), BF), vm((RING, RING, depth, rows), BF),
             act, act, act, act, act, act32, act32, act, act, act,
             vm((step, chan), F32), act, vm((rows, 128), F32), vm((samples, chan), F32),
+            act, act, vm((RING, RING, depth, rows), BF), vm(full, BF),
+            vm((depth, chan), BF), vm((depth, chan), BF),
             vm(emb_table.shape, F32), vm(level_scale.shape, F32),
             vm((depth, chan), F32), vm((depth, chan), F32),
-            vm((4, 4, depth, 640), BF), vm((4, 4, 2, depth, 640), BF),
-            vm((4, depth, 640), BF), vm((4, 2, depth, 640), BF),
-            dma((64,)), dma((64,)), dma((64,)), dma((64,)),
-            dma((4 * BLOCKS,)), dma((4 * BLOCKS,)), dma((9,)),
+            vm((6, 4, depth, 640), BF), vm((6, 4, 2, depth, 640), BF),
+            vm((6, depth, 640), BF), vm((6, 2, depth, 640), BF),
+            dma((64,)), dma((64,)), dma((100,)), dma((100,)),
+            dma((6 * BLOCKS,)), dma((6 * BLOCKS,)), dma((9,)), pltpu.SemaphoreType.REGULAR,
         ],
         compiler_params=pltpu.CompilerParams(
             collective_id=0, has_side_effects=True, vmem_limit_bytes=60 * 1024 * 1024
@@ -518,6 +617,13 @@
         ),
         name="sections",
     )(tokens, grad_out, first_weight, second_weight, emb_table, level_scale, timesteps, levels)
+    return pl.pallas_call(
+        hand_over,
+        out_shape=tuple(jax.ShapeDtypeStruct(r.shape, r.dtype) for r in results),
+        in_specs=[vmspec] * 3,
+        out_specs=(vmspec,) * 3,
+        name="hand_over",
+    )(*results)
 
 
 def solution(mesh):

time: 159 us -> 150 us (0.943)
  local copies, waits for them, and re-layouts: 5.52 us -> 0 us
  Pallas kernels: 151 us -> 148 us
    unnamed x3 -> x0, local copies, waits for them, and re-layouts: 5.52 us -> none
    pallas_call x1, Pallas kernels: 151 us -> 146 us  [local(): pl.pallas_call(kernel, out_shape=(jax.ShapeDtypeStruct((1, depth, chan),...]
    pallas_call x0 -> x1, Pallas kernels: none -> 2.47 us  [local(): pl.pallas_call(hand_over, out_shape=tuple((jax.ShapeDtypeStruct(r.shape,...]
where the time goes in v3:
time: 150 us; the launch traced here: 149 us
  Pallas kernels  148 us (99%)
    pallas_call x1, Pallas kernels, local(): pl.pallas_call(kernel, out_shape=(jax.ShapeDtypeStruct((1, depth, chan),...  146 us

profile of v3, /device:TPU:0, one launch (start us, length us, event | category | flops | bytes accessed | tf_op | source)
XLA Modules:
  0.0 149.4 jit_solution(5394029697992933522)
XLA Ops:
  1.3 145.6 %sections.1 = (f32[1,80,1280]{2,1,0:T(8,128)}, f32[1,80,1280]{2,1,0:T(8,128)}, bf16[1,256,1280]{2,1,0:T(8,128)(2,1)}) custom-call(bf16[256,1280]{1,0:T(8,128)(2,1)} %tok.1, bf16[256,1280]{1,0:T(8,128)(2,1)} %go.1, bf16[1,80,1280]{2,1,0:T(8,128)(2,1)} %w1.1, bf16[1,80,1280]{2,1,0:T(8,128)(2,1)} %w2.1, f32[1000,1280]{1,0:T(8,128)} %emb.1, f32[4,1280]{1,0:T(4,128)} %lvl.1, ...), custom_call_target="tpu_custom_call" | custom-call | flops 5033164800 | bytes 16777216 | tf_op jit(solution)/shard_map/sections/pallas_call | solution.py:588
  146.9 2.5 %hand_over.1 = (f32[1,80,1280]{2,1,0:T(8,128)}, f32[1,80,1280]{2,1,0:T(8,128)}, bf16[1,256,1280]{2,1,0:T(8,128)(2,1)}) custom-call(f32[1,80,1280]{2,1,0:T(8,128)} %get-tuple-element.6.a, f32[1,80,1280]{2,1,0:T(8,128)} %get-tuple-element.7.b, bf16[1,256,1280]{2,1,0:T(8,128)(2,1)} %get-tuple-element.8.c), custom_call_target="tpu_custom_call" | custom-call | tf_op jit(solution)/shard_map/hand_over/pallas_call | solution.py:620

commit v4 on v3

--- a/solution.py
+++ b/solution.py
@@ -12,6 +12,7 @@
 RING = 4
 HELPER = 7
 BLOCKS = 4
+TILE = 128
 HALVES = ((0, 640), (640, 640))
 F32 = jnp.float32
 BF = jnp.bfloat16
@@ -26,8 +27,8 @@
     fg, sg, dxo,
     W1, W2, T1, T2, G1, G2, nT, hT,
     xr, sk, yb, nb, hb, un, sl, gr, gk, dz, dn, dx, rr, cond,
-    hz, gz, hU, G3, accb, accr,
-    embv, lvlv, acc1, acc2, r1, r2, r4, r5,
+    hz, gz, hU, G3, accb, accr, part2,
+    embv, lvlv, r1, r2, r4, r5,
     gsend, grecv, ssend, srecv, psend, precv, lsem, turn_sem,
 ):
     seg = lax.axis_index("segment")
@@ -84,6 +85,12 @@
     def _():
         pl.semaphore_signal(barrier, inc=1, device_id={"segment": jnp.where(seg < 4, seg + 2, seg - 2)})
 
+    helped = jnp.logical_or(seg == 1, seg == HELPER)
+
+    @pl.when(helped)
+    def _():
+        pl.semaphore_signal(barrier, inc=1, device_id={"segment": 1 + HELPER - seg})
+
     far = jnp.logical_or(seg < 3, seg > 4)
 
     @pl.when(far)
@@ -96,12 +103,13 @@
         + (seg > 0).astype(jnp.int32)
         + (seg < SECTIONS - 1).astype(jnp.int32)
         + far.astype(jnp.int32)
-        + relay.astype(jnp.int32),
+        + relay.astype(jnp.int32)
+        + helped.astype(jnp.int32),
     )
     own1.wait()
     own2.wait()
 
-    units = [(w, h) for w in range(2) for h in range(2)]
+    units = [(w, h) for w in range(2) for h in range(2)] + [(2, 1)]
     axes = (("x", "z"), ("z", "x"))
     offs = {"x": at_x, "z": at_z}
     ALL, TOP, LOW = pl.ds(0, 80), pl.ds(0, 48), pl.ds(48, 32)
@@ -112,7 +120,11 @@
 
     def gcopy(u, kind, first, second, part, leg, way):
         w, h = units[u]
-        ref = one((W1, W2)[w], h, offs[axes[h][0]](first), offs[axes[h][1]](second), part)
+        at = (offs[axes[h][0]](first), offs[axes[h][1]](second))
+        if w == 2:
+            ref = part2.at[at[0], at[1], part]
+        else:
+            ref = one((W1, W2)[w], h, *at, part)
         k = u * 16 + kind
         return pltpu.make_async_remote_copy(
             src_ref=ref, dst_ref=ref, send_sem=gsend.at[k], recv_sem=grecv.at[k],
@@ -141,37 +153,101 @@
         second_leg(u, i, 1 if i < 2 else -1).wait_recv()
         second_on(u, i).start()
 
+    PLACES = (0, -1, 1, 2)
+
+    def hand(i, j):
+        at = (at_z(NEAR[i]), at_x(PLACES[j]))
+        there = W2.at[at[0], at[1], :, pl.ds(*HALVES[1])]
+        src, dst, to = (part2.at[at[0], at[1]], there, 1) if i + j else (there, part2.at[z, x], HELPER)
+        k = 80 + 4 * i + j
+        return pltpu.make_async_remote_copy(
+            src_ref=src, dst_ref=dst, send_sem=gsend.at[k], recv_sem=grecv.at[k],
+            device_id={"segment": to},
+        )
+
+    def gather_for_another():
+        hand(0, 0).wait_recv()
+        first_leg(4, 0).start()
+        first_leg(4, 1).start()
+        spread(4, 0)
+        first_leg(4, 0).wait_recv()
+        first_leg(4, 2).start()
+        first_leg(4, 1).wait_recv()
+        first_leg(4, 3).start()
+        spread(4, 1)
+        spread(4, 2)
+        hand(1, 0).start()
+        hand(2, 0).start()
+        pass_on(4, 0)
+        hand(0, 1).start()
+        first_leg(4, 2).wait_recv()
+        first_leg(4, 3).wait_recv()
+        spread(4, 3)
+        hand(3, 0).start()
+        for i in range(1, 4):
+            pass_on(4, i)
+            hand(i, 1 if i < 2 else 2).start()
+        for i in range(4):
+            second_leg(4, i, -1 if i < 2 else 1).wait_recv()
+            hand(i, 2 if i < 2 else 1).start()
+            second_on(4, i).wait_recv()
+            hand(i, 3).start()
+
+    @pl.when(seg == 1)
+    def _():
+        hand(0, 0).start()
+
+    @pl.when(seg == HELPER)
+    def _():
+        gather_for_another()
+
     odd = lax.rem(seg, 2) == 1
 
     @pl.when(odd)
     def _():
         pl.semaphore_wait(turn_sem, 1)
 
-    for u in range(4):
+    def each(do):
+        for u in range(4):
+            if u == 3:
+                pl.when(seg != 1)(lambda: do(3))
+            else:
+                do(u)
+
+    def begin(u):
         first_leg(u, 0).start()
         first_leg(u, 1).start()
-    for u in range(4):
-        spread(u, 0)
-    for u in range(4):
+
+    def onward(u):
         first_leg(u, 0).wait_recv()
         first_leg(u, 2).start()
         first_leg(u, 1).wait_recv()
         first_leg(u, 3).start()
         spread(u, 1)
         spread(u, 2)
-    for u in range(4):
+
+    def across(u):
         pass_on(u, 0)
         first_leg(u, 2).wait_recv()
         first_leg(u, 3).wait_recv()
         spread(u, 3)
 
+    def whole(u):
+        for i in range(4):
+            second_leg(u, i, -1 if i < 2 else 1).wait_recv()
+            second_on(u, i).wait_recv()
+
+    each(begin)
+    each(lambda u: spread(u, 0))
+    each(onward)
+    each(across)
+
     @pl.when(jnp.logical_not(odd))
     def _():
         pl.semaphore_signal(turn_sem, inc=1, device_id={"segment": lax.rem(seg + 1, SECTIONS)})
 
     for i in range(1, 4):
-        for u in range(4):
-            pass_on(u, i)
+        each(lambda u: pass_on(u, i))
 
     table.wait()
     scales.wait()
@@ -187,10 +263,12 @@
     def _():
         go_in.wait()
 
-    for u in range(4):
-        for i in range(4):
-            second_leg(u, i, -1 if i < 2 else 1).wait_recv()
-            second_on(u, i).wait_recv()
+    each(whole)
+
+    @pl.when(seg == 1)
+    def _():
+        for k in range(1, 16):
+            hand(k // 4, k % 4).wait_recv()
 
     def transpose_weights():
         for j in range(0, chan, 256):
@@ -201,16 +279,16 @@
     def _():
         transpose_weights()
 
-    def pcopy(kind, m, src, dst, to):
+    def pcopy(kind, m, src, dst, to, cols=(0, 1280)):
         k = kind * BLOCKS + m
         part = pl.ds(pl.multiple_of(m * step, step), step)
         return pltpu.make_async_remote_copy(
-            src_ref=src.at[part, :], dst_ref=dst.at[part, :],
+            src_ref=src.at[part, pl.ds(*cols)], dst_ref=dst.at[part, pl.ds(*cols)],
             send_sem=psend.at[k], recv_sem=precv.at[k], device_id={"segment": to},
         )
 
-    def y_next(m):
-        return pcopy(0, m, yb, xr, lax.rem(seg + 1, SECTIONS))
+    def y_next(m, i):
+        return pcopy((0, 6)[i], m, yb, xr, lax.rem(seg + 1, SECTIONS), HALVES[i])
 
     def y_skip(m):
         return pcopy(1, m, yb, sk, SECTIONS - 1 - seg)
@@ -246,7 +324,8 @@
 
         @pl.when(seg > 0)
         def _():
-            y_next(m).wait_recv()
+            y_next(m, 0).wait_recv()
+            y_next(m, 1).wait_recv()
 
         @pl.when(seg > 4)
         def _():
@@ -260,21 +339,21 @@
         rr[part, :] = jnp.broadcast_to(r, (step, 128))
         n = (u * r).astype(BF)
         nb[part, :] = n
-        for j in range(0, chan, 256):
-            cols = pl.ds(j, 256)
-            v = dot(n, W1[:, :, :, cols].reshape(chan, 256), ((1,), (0,)))
+        for j in range(0, chan, TILE):
+            cols = pl.ds(j, TILE)
+            v = dot(n, W1[:, :, :, cols].reshape(chan, TILE), ((1,), (0,)))
             s = jax.nn.sigmoid(v)
             hb[part, cols] = (v * s).astype(BF)
             sl[part, cols] = s * (1.0 + v * (1.0 - s))
         h = hb[part, :]
-        for j in range(0, chan, 256):
-            cols = pl.ds(j, 256)
-            v = dot(h, W2[:, :, :, cols].reshape(chan, 256), ((1,), (0,)))
+        for i, half in enumerate(HALVES):
+            cols = pl.ds(*half)
+            v = dot(h, W2[:, :, :, cols].reshape(chan, 640), ((1,), (0,)))
             yb[part, cols] = (xr[part, cols].astype(F32) + v).astype(BF)
 
-        @pl.when(seg < SECTIONS - 1)
-        def _():
-            y_next(m).start()
+            @pl.when(seg < SECTIONS - 1)
+            def _():
+                y_next(m, i).start()
 
         @pl.when(y_direct(m))
         def _():
@@ -323,13 +402,13 @@
             g_out(m).start()
 
         g = gr[part, :]
-        for j in range(0, chan, 256):
-            cols = pl.ds(j, 256)
+        for j in range(0, chan, TILE):
+            cols = pl.ds(j, TILE)
             v = dot(g, T2[:, cols], ((1,), (0,)))
             dz[part, cols] = (v * sl[part, cols]).astype(BF)
         d = dz[part, :]
-        for j in range(0, chan, 256):
-            cols = pl.ds(j, 256)
+        for half in HALVES:
+            cols = pl.ds(*half)
             dn[:, cols] = dot(d, T1[:, cols], ((1,), (0,)))
         nrm = un[part, :]
         v = dn[...]
@@ -438,7 +517,7 @@
             total = block(u, 0, 0)[...].astype(F32)
             for value in (r2[u, i, 0], r2[u, i, 1], r5[u, 0], r5[u, 1]):
                 total = total + value.astype(F32)
-            to = (acc1, acc2, accb)[w]
+            to = (fg.at[0], sg.at[0], accb)[w]
             to[:, pl.ds(*HALVES[h])] = total.astype(to.dtype)
 
     def ours(u, do):
@@ -478,28 +557,27 @@
         result(1).start()
 
     own, more = range(4), range(4, 6)
-    group(own, (leave, 0), (leave, 2))
-    group(own, (go_beside, 0), (go_beside, 2))
-    group(own, (leave, 1), (leave, 3))
+    group(own, (leave, 0))
+    group(own, (leave, 2))
+    group(own, (go_beside, 0))
+    group(own, (leave, 1))
+    group(own, (go_beside, 2))
     group(own, (arrive, 0))
-    group(own, (go_beside, 1), (go_beside, 3))
+    group(own, (leave, 3))
+    group(own, (go_beside, 1))
     group(own, (arrive, 2))
+    group(own, (go_beside, 3))
+    group(own, (arrive, 1))
     helper(take_over)
-    group(own, (arrive, 1))
     helper(lambda: group(more, (go_beside, 0), (go_beside, 2), (arrive, 0)))
+    helper(give_back)
     group(own, (arrive, 3))
-    helper(give_back)
 
     @pl.when(seg == 0)
     def _():
         for h in range(2):
             result(h).wait_recv()
-        acc2[...] = accr[...].astype(F32)
-
-    out1 = pltpu.make_async_copy(acc1, fg.at[0], lsem.at[7])
-    out2 = pltpu.make_async_copy(acc2, sg.at[0], lsem.at[8])
-    out1.start()
-    out2.start()
+        sg[0] = accr[...].astype(F32)
 
     def scattered(u):
         for k in range(4):
@@ -510,13 +588,26 @@
             last_opposite(u, way).wait_send()
             last_beside(u, way).wait_send()
 
-    for u in range(4):
+    def gathered(u):
         for k in range(4):
             first_leg(u, k).wait_send()
             second_leg(u, k, 1).wait_send()
             second_leg(u, k, -1).wait_send()
             second_on(u, k).wait_send()
+
+    each(gathered)
+    for u in range(4):
         ours(u, lambda: scattered(u))
+
+    @pl.when(seg == 1)
+    def _():
+        hand(0, 0).wait_send()
+
+    @pl.when(seg == HELPER)
+    def _():
+        gathered(4)
+        for k in range(1, 16):
+            hand(k // 4, k % 4).wait_send()
 
     @pl.when(seg == HELPER)
     def _():
@@ -543,7 +634,8 @@
     def sent(m, carry):
         @pl.when(seg < SECTIONS - 1)
         def _():
-            y_next(m).wait_send()
+            y_next(m, 0).wait_send()
+            y_next(m, 1).wait_send()
 
         @pl.when(y_direct(m))
         def _():
@@ -561,14 +653,6 @@
 
     lax.fori_loop(0, BLOCKS, sent, 0)
     dx_out.wait()
-    out1.wait()
-    out2.wait()
-
-
-def hand_over(a, b, c, out_a, out_b, out_c):
-    out_a[...] = a[...]
-    out_b[...] = b[...]
-    out_c[...] = c[...]
 
 
 def local(tokens, grad_out, first_weight, second_weight, emb_table, level_scale, timesteps, levels):
@@ -585,15 +669,15 @@
     vmspec = pl.BlockSpec(memory_space=pltpu.VMEM)
     smem = pl.BlockSpec(memory_space=pltpu.SMEM)
     macs = 6 * rows * chan * chan
-    results = pl.pallas_call(
+    return pl.pallas_call(
         kernel,
         out_shape=(
-            jax.ShapeDtypeStruct((1, depth, chan), F32),
-            jax.ShapeDtypeStruct((1, depth, chan), F32),
-            jax.ShapeDtypeStruct((1, rows, chan), BF),
+            vm((1, depth, chan), F32),
+            vm((1, depth, chan), F32),
+            vm((1, rows, chan), BF),
         ),
         in_specs=[anyspec] * 6 + [smem] * 2,
-        out_specs=(anyspec,) * 3,
+        out_specs=(vmspec,) * 3,
         scratch_shapes=[
             vm(full, BF), vm(full, BF), vm((chan, chan), BF), vm((chan, chan), BF),
             vm(full, BF), vm(full, BF),
@@ -601,13 +685,12 @@
             act, act, act, act, act, act32, act32, act, act, act,
             vm((step, chan), F32), act, vm((rows, 128), F32), vm((samples, chan), F32),
             act, act, vm((RING, RING, depth, rows), BF), vm(full, BF),
-            vm((depth, chan), BF), vm((depth, chan), BF),
+            vm((depth, chan), BF), vm((depth, chan), BF), vm((RING, RING, depth, 640), BF),
             vm(emb_table.shape, F32), vm(level_scale.shape, F32),
-            vm((depth, chan), F32), vm((depth, chan), F32),
             vm((6, 4, depth, 640), BF), vm((6, 4, 2, depth, 640), BF),
             vm((6, depth, 640), BF), vm((6, 2, depth, 640), BF),
-            dma((64,)), dma((64,)), dma((100,)), dma((100,)),
-            dma((6 * BLOCKS,)), dma((6 * BLOCKS,)), dma((9,)), pltpu.SemaphoreType.REGULAR,
+            dma((96,)), dma((96,)), dma((100,)), dma((100,)),
+            dma((7 * BLOCKS,)), dma((7 * BLOCKS,)), dma((7,)), pltpu.SemaphoreType.REGULAR,
         ],
         compiler_params=pltpu.CompilerParams(
             collective_id=0, has_side_effects=True, vmem_limit_bytes=60 * 1024 * 1024
@@ -617,13 +700,6 @@
         ),
         name="sections",
     )(tokens, grad_out, first_weight, second_weight, emb_table, level_scale, timesteps, levels)
-    return pl.pallas_call(
-        hand_over,
-        out_shape=tuple(jax.ShapeDtypeStruct(r.shape, r.dtype) for r in results),
-        in_specs=[vmspec] * 3,
-        out_specs=(vmspec,) * 3,
-        name="hand_over",
-    )(*results)
 
 
 def solution(mesh):

time: 150 us -> 145 us (0.967)
  Pallas kernels: 148 us -> 141 us
  local copies, waits for them, and re-layouts: 0 us -> 2.34 us
    pallas_call x2 -> x1, Pallas kernels: 148 us -> 141 us  [local(): pl.pallas_call(kernel, out_shape=(vm((1, depth, chan), F32), vm((1, depth...]
    unnamed x0 -> x3, local copies, waits for them, and re-layouts: none -> 2.34 us
where the time goes in v4:
time: 145 us
  Pallas kernels  141 us (97%)
  local copies, waits for them, and re-layouts  2.34 us (2%)
    pallas_call x1, Pallas kernels, local(): pl.pallas_call(kernel, out_shape=(vm((1, depth, chan), F32), vm((1, depth...  141 us

profile of v4, /device:TPU:0, one launch (start us, length us, event | category | flops | bytes accessed | tf_op | source)
XLA Modules:
  0.0 144.8 jit_solution(17251482149320960144)
XLA Ops:
  1.3 141.1 %sections.1 = (f32[1,80,1280]{2,1,0:T(8,128)S(1)}, f32[1,80,1280]{2,1,0:T(8,128)S(1)}, bf16[1,256,1280]{2,1,0:T(8,128)(2,1)S(1)}) custom-call(bf16[256,1280]{1,0:T(8,128)(2,1)} %tok.1, bf16[256,1280]{1,0:T(8,128)(2,1)} %go.1, bf16[1,80,1280]{2,1,0:T(8,128)(2,1)} %w1.1, bf16[1,80,1280]{2,1,0:T(8,128)(2,1)} %w2.1, f32[1000,1280]{1,0:T(8,128)} %emb.1, ...), custom_call_target="tpu_custom_call" | custom-call | flops 5033164800 | bytes 16777216 | tf_op jit(solution)/shard_map/sections/pallas_call | solution.py:672
  142.4 0.8 copy.14
  143.2 0.8 copy.15
  143.9 0.8 copy.16

commit v5 on v4

--- a/solution.py
+++ b/solution.py
@@ -133,9 +133,12 @@
 
     NEAR = (0, -1, 1, 2)
 
+    def share(u, way):
+        return TOP if (way > 0) == (u % 4 < 2) else LOW
+
     def first_leg(u, kind):
         return gcopy(
-            u, kind, (0, 0, -1, 1)[kind], 0, (ALL, ALL, TOP, LOW)[kind], 0, (1, -1, 1, -1)[kind]
+            u, kind, (0, 0, -1, 1)[kind], 0, (ALL, ALL, share(u, 1), share(u, -1))[kind], 0, (1, -1, 1, -1)[kind]
         )
 
     def second_leg(u, i, way):
@@ -240,11 +243,11 @@
     each(begin)
     each(lambda u: spread(u, 0))
     each(onward)
+    @pl.when(jnp.logical_not(odd))
+    def _():
+        pl.semaphore_signal(turn_sem, inc=1, device_id={"segment": lax.rem(seg + 1, SECTIONS)})
+
     each(across)
-
-    @pl.when(jnp.logical_not(odd))
-    def _():
-        pl.semaphore_signal(turn_sem, inc=1, device_id={"segment": lax.rem(seg + 1, SECTIONS)})
 
     for i in range(1, 4):
         each(lambda u: pass_on(u, i))
@@ -473,7 +476,7 @@
         return scopy(u, k, block(u, FAR[i], way), r2.at[u, i, int(way < 0)], 1, way)
 
     def last_opposite(u, way):
-        part = TOP if way > 0 else LOW
+        part = share(u, way)
         return scopy(u, 12 + (way < 0), block(u, 2, 0, part), r4.at[u, part], 0, way)
 
     def last_beside(u, way):
@@ -506,7 +509,7 @@
             last_opposite(u, -1).start()
         elif i < 3:
             way = FAR[i]
-            part = TOP if way > 0 else LOW
+            part = share(u, way)
             last_opposite(u, way).wait_recv()
             add(block(u, way, 0, part), r4[u, part])
             last_beside(u, way).start()

time: 145 us -> 143 us (0.986)
  Pallas kernels: 141 us -> 139 us
    pallas_call x1, Pallas kernels: 141 us -> 139 us  [local(): pl.pallas_call(kernel, out_shape=(vm((1, depth, chan), F32), vm((1, depth...]
where the time goes in v5:
time: 143 us; the launch traced here: 142 us
  Pallas kernels  139 us (97%)
  local copies, waits for them, and re-layouts  2.34 us (2%)
    pallas_call x1, Pallas kernels, local(): pl.pallas_call(kernel, out_shape=(vm((1, depth, chan), F32), vm((1, depth...  139 us

profile of v5, /device:TPU:0, one launch (start us, length us, event | category | flops | bytes accessed | tf_op | source)
XLA Modules:
  0.0 142.4 jit_solution(14068424564801899218)
XLA Ops:
  1.3 138.8 %sections.1 = (f32[1,80,1280]{2,1,0:T(8,128)S(1)}, f32[1,80,1280]{2,1,0:T(8,128)S(1)}, bf16[1,256,1280]{2,1,0:T(8,128)(2,1)S(1)}) custom-call(bf16[256,1280]{1,0:T(8,128)(2,1)} %tok.1, bf16[256,1280]{1,0:T(8,128)(2,1)} %go.1, bf16[1,80,1280]{2,1,0:T(8,128)(2,1)} %w1.1, bf16[1,80,1280]{2,1,0:T(8,128)(2,1)} %w2.1, f32[1000,1280]{1,0:T(8,128)} %emb.1, ...), custom_call_target="tpu_custom_call" | custom-call | flops 5033164800 | bytes 16777216 | tf_op jit(solution)/shard_map/sections/pallas_call | solution.py:675
  140.1 0.8 copy.14
  140.8 0.8 copy.15
  141.6 0.8 copy.16

commit v6 on v5

--- a/solution.py
+++ b/solution.py
@@ -550,14 +550,17 @@
             g_out(m).wait_recv()
         hU[...] = hz[...].T.reshape(hU.shape)
         group(more, (leave, 0), (leave, 2))
+        group(more, (go_beside, 0), (go_beside, 2))
         group(more, (leave, 1), (leave, 3))
+        group(more, (arrive, 0))
 
     def give_back():
         group(more, (go_beside, 1), (go_beside, 3))
-        for i in (2, 1, 3):
-            group(more, (arrive, i))
-        result(0).start()
-        result(1).start()
+        group(more, (arrive, 2))
+        group(more, (arrive, 1))
+        for h in range(2):
+            arrive(4 + h, 3)
+            result(h).start()
 
     own, more = range(4), range(4, 6)
     group(own, (leave, 0))
@@ -572,7 +575,6 @@
     group(own, (go_beside, 3))
     group(own, (arrive, 1))
     helper(take_over)
-    helper(lambda: group(more, (go_beside, 0), (go_beside, 2), (arrive, 0)))
     helper(give_back)
     group(own, (arrive, 3))
 

time: 143 us -> 141 us (0.986)
  Pallas kernels: 139 us -> 136 us
    pallas_call x1, Pallas kernels: 139 us -> 136 us  [local(): pl.pallas_call(kernel, out_shape=(vm((1, depth, chan), F32), vm((1, depth...]
where the time goes in v6:
time: 141 us; the launch traced here: 140 us
  Pallas kernels  136 us (96%)
  local copies, waits for them, and re-layouts  2.34 us (2%)
    pallas_call x1, Pallas kernels, local(): pl.pallas_call(kernel, out_shape=(vm((1, depth, chan), F32), vm((1, depth...  136 us

profile of v6, /device:TPU:0, one launch (start us, length us, event | category | flops | bytes accessed | tf_op | source)
XLA Modules:
  0.0 139.7 jit_solution(1790337539106945859)
XLA Ops:
  1.3 136.1 %sections.1 = (f32[1,80,1280]{2,1,0:T(8,128)S(1)}, f32[1,80,1280]{2,1,0:T(8,128)S(1)}, bf16[1,256,1280]{2,1,0:T(8,128)(2,1)S(1)}) custom-call(bf16[256,1280]{1,0:T(8,128)(2,1)} %tok.1, bf16[256,1280]{1,0:T(8,128)(2,1)} %go.1, bf16[1,80,1280]{2,1,0:T(8,128)(2,1)} %w1.1, bf16[1,80,1280]{2,1,0:T(8,128)(2,1)} %w2.1, f32[1000,1280]{1,0:T(8,128)} %emb.1, ...), custom_call_target="tpu_custom_call" | custom-call | flops 5033164800 | bytes 16777216 | tf_op jit(solution)/shard_map/sections/pallas_call | solution.py:677
  137.4 0.8 copy.14
  138.2 0.8 copy.15
  138.9 0.8 copy.16

commit v7 on v6

--- a/solution.py
+++ b/solution.py
@@ -26,7 +26,7 @@
     tok, go, w1, w2, emb, lvl, ts, lv,
     fg, sg, dxo,
     W1, W2, T1, T2, G1, G2, nT, hT,
-    xr, sk, yb, nb, hb, un, sl, gr, gk, dz, dn, dx, rr, cond,
+    xr, sk, yb, nb, hb, un, sl, zb, gr, gk, dz, dx, rr, cond,
     hz, gz, hU, G3, accb, accr, part2,
     embv, lvlv, r1, r2, r4, r5,
     gsend, grecv, ssend, srecv, psend, precv, lsem, turn_sem,
@@ -249,8 +249,7 @@
 
     each(across)
 
-    for i in range(1, 4):
-        each(lambda u: pass_on(u, i))
+    each(lambda u: [pass_on(u, i) for i in range(1, 4)] and None)
 
     table.wait()
     scales.wait()
@@ -296,8 +295,8 @@
     def y_skip(m):
         return pcopy(1, m, yb, sk, SECTIONS - 1 - seg)
 
-    def g_next(m):
-        return pcopy(2, m, dx, gr, lax.rem(seg + SECTIONS - 1, SECTIONS))
+    def g_next(m, i):
+        return pcopy((2, 7)[i], m, dx, gr, lax.rem(seg + SECTIONS - 1, SECTIONS), HALVES[i])
 
     def g_skip(m):
         return pcopy(3, m, dx, gk, SECTIONS - 1 - seg)
@@ -346,6 +345,7 @@
             cols = pl.ds(j, TILE)
             v = dot(n, W1[:, :, :, cols].reshape(chan, TILE), ((1,), (0,)))
             s = jax.nn.sigmoid(v)
+            zb[part, cols] = v
             hb[part, cols] = (v * s).astype(BF)
             sl[part, cols] = s * (1.0 + v * (1.0 - s))
         h = hb[part, :]
@@ -393,7 +393,8 @@
 
         @pl.when(seg < SECTIONS - 1)
         def _():
-            g_next(m).wait_recv()
+            g_next(m, 0).wait_recv()
+            g_next(m, 1).wait_recv()
 
         @pl.when(seg < 3)
         def _():
@@ -405,23 +406,24 @@
             g_out(m).start()
 
         g = gr[part, :]
+        along = jnp.zeros((step, TILE), F32)
         for j in range(0, chan, TILE):
             cols = pl.ds(j, TILE)
             v = dot(g, T2[:, cols], ((1,), (0,)))
-            dz[part, cols] = (v * sl[part, cols]).astype(BF)
+            d = (v * sl[part, cols]).astype(BF)
+            dz[part, cols] = d
+            along = along + d.astype(F32) * zb[part, cols]
+        along = jnp.sum(along, axis=-1, keepdims=True) * (1.0 / chan)
         d = dz[part, :]
-        for half in HALVES:
+        r = rr[part, pl.ds(0, 1)]
+        for i, half in enumerate(HALVES):
             cols = pl.ds(*half)
-            dn[:, cols] = dot(d, T1[:, cols], ((1,), (0,)))
-        nrm = un[part, :]
-        v = dn[...]
-        along = jnp.mean(nrm * v, axis=-1, keepdims=True)
-        r = rr[part, pl.ds(0, 1)]
-        dx[part, :] = (g.astype(F32) + r * (v - nrm * along)).astype(BF)
-
-        @pl.when(seg > 0)
-        def _():
-            g_next(m).start()
+            v = dot(d, T1[:, cols], ((1,), (0,)))
+            dx[part, cols] = (gr[part, cols].astype(F32) + r * (v - un[part, cols] * along)).astype(BF)
+
+            @pl.when(seg > 0)
+            def _():
+                g_next(m, i).start()
 
         @pl.when(g_direct(m))
         def _():
@@ -566,13 +568,13 @@
     group(own, (leave, 0))
     group(own, (leave, 2))
     group(own, (go_beside, 0))
+    group(own, (go_beside, 2))
     group(own, (leave, 1))
-    group(own, (go_beside, 2))
+    group(own, (leave, 3))
     group(own, (arrive, 0))
-    group(own, (leave, 3))
     group(own, (go_beside, 1))
+    group(own, (go_beside, 3))
     group(own, (arrive, 2))
-    group(own, (go_beside, 3))
     group(own, (arrive, 1))
     helper(take_over)
     helper(give_back)
@@ -648,7 +650,8 @@
 
         @pl.when(seg > 0)
         def _():
-            g_next(m).wait_send()
+            g_next(m, 0).wait_send()
+            g_next(m, 1).wait_send()
 
         @pl.when(g_direct(m))
         def _():
@@ -687,15 +690,15 @@
             vm(full, BF), vm(full, BF), vm((chan, chan), BF), vm((chan, chan), BF),
             vm(full, BF), vm(full, BF),
             vm((RING, RING, depth, rows), BF), vm((RING, RING, depth, rows), BF),
-            act, act, act, act, act, act32, act32, act, act, act,
-            vm((step, chan), F32), act, vm((rows, 128), F32), vm((samples, chan), F32),
+            act, act, act, act, act, act32, act32, act32, act, act, act,
+            act, vm((rows, 128), F32), vm((samples, chan), F32),
             act, act, vm((RING, RING, depth, rows), BF), vm(full, BF),
             vm((depth, chan), BF), vm((depth, chan), BF), vm((RING, RING, depth, 640), BF),
             vm(emb_table.shape, F32), vm(level_scale.shape, F32),
             vm((6, 4, depth, 640), BF), vm((6, 4, 2, depth, 640), BF),
             vm((6, depth, 640), BF), vm((6, 2, depth, 640), BF),
             dma((96,)), dma((96,)), dma((100,)), dma((100,)),
-            dma((7 * BLOCKS,)), dma((7 * BLOCKS,)), dma((7,)), pltpu.SemaphoreType.REGULAR,
+            dma((8 * BLOCKS,)), dma((8 * BLOCKS,)), dma((7,)), pltpu.SemaphoreType.REGULAR,
         ],
         compiler_params=pltpu.CompilerParams(
             collective_id=0, has_side_effects=True, vmem_limit_bytes=60 * 1024 * 1024

time: 141 us -> 141 us (level)
  no operation moved by 1% of the time
where the time goes in v7:
time: 141 us; the launch traced here: 140 us
  Pallas kernels  137 us (97%)
  local copies, waits for them, and re-layouts  2.34 us (2%)
    pallas_call x1, Pallas kernels, local(): pl.pallas_call(kernel, out_shape=(vm((1, depth, chan), F32), vm((1, depth...  137 us

profile of v7, /device:TPU:0, one launch (start us, length us, event | category | flops | bytes accessed | tf_op | source)
XLA Modules:
  0.0 140.3 jit_solution(4998155023711418842)
XLA Ops:
  1.3 136.6 %sections.1 = (f32[1,80,1280]{2,1,0:T(8,128)S(1)}, f32[1,80,1280]{2,1,0:T(8,128)S(1)}, bf16[1,256,1280]{2,1,0:T(8,128)(2,1)S(1)}) custom-call(bf16[256,1280]{1,0:T(8,128)(2,1)} %tok.1, bf16[256,1280]{1,0:T(8,128)(2,1)} %go.1, bf16[1,80,1280]{2,1,0:T(8,128)(2,1)} %w1.1, bf16[1,80,1280]{2,1,0:T(8,128)(2,1)} %w2.1, f32[1000,1280]{1,0:T(8,128)} %emb.1, ...), custom_call_target="tpu_custom_call" | custom-call | flops 5033164800 | bytes 16777216 | tf_op jit(solution)/shard_map/sections/pallas_call | solution.py:680
  137.9 0.8 copy.14
  138.7 0.8 copy.15
  139.4 0.8 copy.16
